TPU v7x, 512 devices: a whole 4x8x8 slice. The times are simulated.
512 devices in a mesh: row: 32 (over x, y_lo, core), col: 16 (over y_hi, z).
Axes of the slice: x: 4, y: 8 (y_hi: 2, y_lo: 4; y = y_hi * 4 + y_lo), z: 8, core: 2. Of those that a mesh axis runs over, the one named last changes fastest.
Arguments:
- tokens: bfloat16 [1024, 6144], P('row', 'col'), may hold values from -6 to 6
- grad_out: bfloat16 [1024, 6144], P('row', 'col'), may hold values from -6 to 6
- gate_pre: bfloat16 [1024, 24576], P('col', 'row'), may hold values from -8 to 8
- up_pre: bfloat16 [1024, 24576], P('col', 'row'), may hold values from -6 to 6
- w_gate: bfloat16 [6144, 24576], P('col', 'row'), may hold values from -0.078125 to 0.078125
- w_up: bfloat16 [6144, 24576], P('col', 'row'), may hold values from -0.078125 to 0.078125
- w_down: bfloat16 [24576, 6144], P('row', 'col'), may hold values from -0.0390625 to 0.0390625
Outputs:
- grad_tokens: bfloat16 [1024, 6144], P('row', 'col')
- grad_gate: bfloat16 [6144, 24576], P('col', 'row')
- grad_up: bfloat16 [6144, 24576], P('col', 'row')
- grad_down: bfloat16 [24576, 6144], P('row', 'col')
All inputs are finite; a program needn't handle non-finite values.
Results may differ from a plain program's by a relative error of at most 0.0049.
Values may be sent and summed in bfloat16 or wider, within the bound.
A program may use at most 64 MiB of HBM per device.

v0:
```python
import jax
import jax.numpy as jnp
from jax import lax
from jax.sharding import PartitionSpec as P


def contract(left_side, right_side, left_dim, right_dim):
    return lax.dot_general(
        left_side,
        right_side,
        (((left_dim,), (right_dim,)), ((), ())),
        preferred_element_type=jnp.float32,
    )


def swiglu_backward(grad_hidden, gate_pre, up_pre):
    gate_value = gate_pre.astype(jnp.float32)
    up_value = up_pre.astype(jnp.float32)
    sigmoid_gate = jax.nn.sigmoid(gate_value)
    silu_gate = gate_value * sigmoid_gate
    hidden = (silu_gate * up_value).astype(jnp.bfloat16)
    grad_up = (grad_hidden * silu_gate).astype(jnp.bfloat16)
    grad_gate = (
        grad_hidden * up_value * sigmoid_gate * (1.0 + gate_value * (1.0 - sigmoid_gate))
    ).astype(jnp.bfloat16)
    return (hidden, grad_gate, grad_up)


def on_device(tokens, grad_out, gate_pre, up_pre, w_gate, w_up, w_down):
    grad_full, tokens_full = (
        lax.all_gather(grad_out, "row", axis=0, tiled=True),
        lax.all_gather(tokens, "row", axis=0, tiled=True),
    )
    grad_hidden = lax.psum_scatter(
        contract(grad_full, w_down, 1, 1), "col", scatter_dimension=0, tiled=True
    )
    hidden_share, gate_share, up_share = swiglu_backward(grad_hidden, gate_pre, up_pre)
    hidden_full, gate_grad_full, up_grad_full = (
        lax.all_gather(hidden_share, "col", axis=0, tiled=True),
        lax.all_gather(gate_share, "col", axis=0, tiled=True),
        lax.all_gather(up_share, "col", axis=0, tiled=True),
    )
    grad_down = contract(hidden_full, grad_full, 0, 0).astype(jnp.bfloat16)
    grad_gate = contract(tokens_full, gate_grad_full, 0, 0).astype(jnp.bfloat16)
    grad_up = contract(tokens_full, up_grad_full, 0, 0).astype(jnp.bfloat16)
    grad_tokens = lax.psum_scatter(
        contract(gate_grad_full, w_gate, 1, 1) + contract(up_grad_full, w_up, 1, 1),
        "row",
        scatter_dimension=0,
        tiled=True,
    ).astype(jnp.bfloat16)
    return (grad_tokens, grad_gate, grad_up, grad_down)


def solution(mesh):
    return jax.shard_map(
        on_device,
        mesh=mesh,
        in_specs=(
            P("row", "col"),
            P("row", "col"),
            P("col", "row"),
            P("col", "row"),
            P("col", "row"),
            P("col", "row"),
            P("row", "col"),
        ),
        out_specs=(P("row", "col"), P("col", "row"), P("col", "row"), P("row", "col")),
        check_vma=False,
    )
```

profile of v0, /device:TPU:1, one launch (start us, length us, event | category | flops | bytes accessed | tf_op | source)
XLA Modules:
  0.0 729.0 jit_solution(9628554661551148043)
XLA Ops:
  7.2 0.0 reduce-scatter.3.cloned.1.call-start
  7.2 48.6 %all_gather.15 = bf16[1024,384]{1,0:T(8,128)(2,1)S(1)} all-gather(bf16[32,384]{1,0:T(8,128)(2,1)} %param.8), channel_id=1, replica_groups=mesh['row'=32,'col'=16] {'row'}, dimensions={0}, use_global_device_ids=true | all-gather | bytes 811008 | tf_op jit(solution)/shard_map/all_gather | solution.py:31
  55.9 2.7 fusion.10
  58.5 0.0 all-gather.4.cloned.1.call-start
  58.6 224.5 %reduce-scatter.3.cloned.1.call-done = f32[64,768]{1,0:T(8,128)} async-done(((f32[1024,768]{1,0:T(8,128)}), f32[64,768]{1,0:T(8,128)}) %reduce-scatter.3.cloned.1.call-update) | async-done | bytes 196624 | tf_op jit(solution)/shard_map/reduce_scatter | solution.py:34
  283.1 1.7 multiply_convert_fusion
  284.8 0.0 all-gather.6.cloned.1.call-start
  284.9 0.7 all-gather.6.cloned.1.call-update
  285.6 0.5 all-gather.8.cloned.1.call-update
  286.2 0.0 reduce-scatter.5.cloned.1.call-start
  286.2 93.3 %all-gather.4.cloned.1.call-done = bf16[1024,768]{1,0:T(8,128)(2,1)} async-done(((bf16[64,768]{1,0:T(8,128)(2,1)}), bf16[1024,768]{1,0:T(8,128)(2,1)}) %all-gather.4.cloned.1.call-update) | async-done | bytes 1572880 | tf_op jit(solution)/shard_map/all_gather | solution.py:40
  379.5 2.4 fusion.11
  381.9 94.7 %all-gather.6.cloned.1.call-done = bf16[1024,768]{1,0:T(8,128)(2,1)} async-done(((bf16[64,768]{1,0:T(8,128)(2,1)}), bf16[1024,768]{1,0:T(8,128)(2,1)}) %all-gather.6.cloned.1.call-update) | async-done | bytes 1572880 | tf_op jit(solution)/shard_map/all_gather | solution.py:41
  476.6 3.7 convolution_add_fusion
  480.4 50.9 %all_gather.18 = bf16[1024,384]{1,0:T(8,128)(2,1)S(1)} all-gather(bf16[32,384]{1,0:T(8,128)(2,1)S(1)} %copy-done.6), channel_id=1, replica_groups=mesh['row'=32,'col'=16] {'row'}, dimensions={0}, use_global_device_ids=true | all-gather | bytes 811008 | tf_op jit(solution)/shard_map/all_gather | solution.py:32
  531.3 0.9 copy-done.2
  532.2 1.0 fusion
  533.2 1.1 copy.11
  534.3 2.6 fusion.1
  536.9 1.1 copy.12
  538.0 34.1 %all-gather.8.cloned.1.call-done = bf16[1024,768]{1,0:T(8,128)(2,1)} async-done(((bf16[64,768]{1,0:T(8,128)(2,1)}), bf16[1024,768]{1,0:T(8,128)(2,1)}) %all-gather.8.cloned.1.call-update) | async-done | bytes 1572880 | tf_op jit(solution)/shard_map/all_gather | solution.py:39
  572.1 3.2 convolution_convert_fusion
  575.4 145.7 %reduce-scatter.5.cloned.1.call-done = f32[32,384]{1,0:T(8,128)} async-done(((f32[1024,384]{1,0:T(8,128)}), f32[32,384]{1,0:T(8,128)}) %reduce-scatter.5.cloned.1.call-update) | async-done | bytes 49168 | tf_op jit(solution)/shard_map/reduce_scatter | solution.py:46
  721.1 1.4 convert_element_type.37
  (17 shorter events, 0.1 us)
Async XLA Ops:
  7.2 48.7 %copy-start = (bf16[768,384]{1,0:T(8,128)(2,1)S(1)}, bf16[768,384]{1,0:T(8,128)(2,1)}, u32[]{:S(2)}) copy-start(bf16[768,384]{1,0:T(8,128)(2,1)} %param.13) | copy-start | bytes 1769476
  7.2 275.9 %reduce-scatter.3.cloned.1.call-start = ((), (), s32[]{:S(2)}) async-start(), calls=%async_computation.2 | async-start | bytes 3342336 | tf_op jit(solution)/shard_map/reduce_scatter | solution.py:34
  58.5 224.6 %copy-start.4 = (bf16[64,768]{1,0:T(8,128)(2,1)S(1)}, bf16[64,768]{1,0:T(8,128)(2,1)}, u32[]{:S(2)}) copy-start(bf16[64,768]{1,0:T(8,128)(2,1)} %param.9) | copy-start | bytes 294916
  58.5 224.6 %copy-start.5 = (bf16[64,768]{1,0:T(8,128)(2,1)S(1)}, bf16[64,768]{1,0:T(8,128)(2,1)}, u32[]{:S(2)}) copy-start(bf16[64,768]{1,0:T(8,128)(2,1)} %param.10) | copy-start | bytes 294916
  58.5 321.0 %copy-start.3 = (bf16[384,768]{1,0:T(8,128)(2,1)S(1)}, bf16[384,768]{1,0:T(8,128)(2,1)}, u32[]{:S(2)}) copy-start(bf16[384,768]{1,0:T(8,128)(2,1)} %param.11) | copy-start | bytes 1769476
  58.5 321.0 %all-gather.4.cloned.1.call-start = ((), (), s32[]{:S(2)}) async-start(), calls=%async_computation.3 | async-start | bytes 1671168 | tf_op jit(solution)/shard_map/all_gather | solution.py:40
  284.8 191.8 %all-gather.6.cloned.1.call-start = ((), (), s32[]{:S(2)}) async-start(), calls=%async_computation.4 | async-start | bytes 1671168 | tf_op jit(solution)/shard_map/all_gather | solution.py:41
  285.6 286.5 %all-gather.8.cloned.1.call-start = ((), (), s32[]{:S(2)}) async-start(), calls=%async_computation.6 | async-start | bytes 1671168 | tf_op jit(solution)/shard_map/all_gather | solution.py:39
  286.2 434.9 %reduce-scatter.5.cloned.1.call-start = ((), (), s32[]{:S(2)}) async-start(), calls=%async_computation.5 | async-start | bytes 1622016 | tf_op jit(solution)/shard_map/reduce_scatter | solution.py:46
  476.6 3.7 copy-start.6
  480.3 51.9 %copy-start.1 = (bf16[1024,768]{1,0:T(8,128)(2,1)S(1)}, bf16[1024,768]{1,0:T(8,128)(2,1)}, u32[]{:S(2)}) copy-start(bf16[1024,768]{1,0:T(8,128)(2,1)} %all-gather.4.cloned.1.call-done) | copy-start | bytes 4718596
  531.3 0.9 copy-start.2
Sparse Core Ops, SparseCore 0:
  58.7 224.3 reduce-scatter.2
  287.3 92.1 all-gather.3
  383.8 92.8 all-gather.5
  480.1 91.9 all-gather.7
  575.0 146.0 reduce-scatter.4
where the time goes:
time: 732 us; the launch traced here: 729 us
  waiting for transfers between devices  594 us (81%)
  blocking collectives  99.6 us (14%)
  matrix products  15.6 us (2%)
  between operations  13.8 us (2%)
    reduce_scatter x1, waiting for transfers between devices, on_device(): lax.psum_scatter(contract(grad_full, w_down, 1, 1), 'col', scatter_dimens...  224 us
    reduce_scatter x1, waiting for transfers between devices, on_device(): lax.psum_scatter(contract(gate_grad_full, w_gate, 1, 1) + contract(up_gra...  146 us
    all_gather x1, waiting for transfers between devices, on_device(): lax.all_gather(up_share, 'col', axis=0, tiled=True)  94.7 us
    all_gather x1, waiting for transfers between devices, on_device(): lax.all_gather(gate_share, 'col', axis=0, tiled=True)  93.3 us
    all_gather x1, blocking collectives, on_device(): lax.all_gather(tokens, 'row', axis=0, tiled=True)  50.9 us
    all_gather x1, blocking collectives, on_device(): lax.all_gather(grad_out, 'row', axis=0, tiled=True)  48.6 us
    all_gather x1, waiting for transfers between devices, on_device(): lax.all_gather(hidden_share, 'col', axis=0, tiled=True)  34.1 us
    dot_general x6, matrix products, contract(): lax.dot_general(left_side, right_side, (((left_dim,), (right_dim,)), ((),...  15.6 us
  transfers between devices with their start and end apart: 5, of which 5 were waited for; matrix products, arithmetic and copies ran while one was open for 2% of the time, Pallas kernels for 0%

commit v1 on v0

v1 whole, which is shorter than its diff:
```python
import functools

import jax
import jax.numpy as jnp
from jax import lax
from jax.experimental import pallas as pl
from jax.experimental.pallas import tpu as pltpu
from jax.sharding import PartitionSpec as P

MESH = pl.DeviceIdType.MESH
F32 = jnp.float32
BF16 = jnp.bfloat16
NX, NY, NC = 4, 4, 2
NH, NZ = 2, 8
ROWS = 16
COPIES = 110


def dot(left, right, left_dim, right_dim):
    return lax.dot_general(
        left, right, (((left_dim,), (right_dim,)), ((), ())), preferred_element_type=F32
    )


def kernel(
    tok_ref, go_ref, gate_ref, up_ref, wg_ref, wu_ref, wd_ref,
    out_gt, out_gg, out_gu, out_gd,
    tok_all, go_all, acts, wg, wu, wd, part, rs_send, rs_recv, swap_send, swap_recv,
    grad_h, silu, slope, hidden, gate_grad, up_grad, tok_t, pair_sum, core_send, core_recv,
    x_send, x_recv, x_own, y_send, y_recv, st_gg, st_gu, st_gd,
    send, recv, core_send_sem, core_recv_sem, x_send_sem, x_recv_sem, here,
):
    row, col = lax.axis_index("row"), lax.axis_index("col")
    x, yl, core = row // (NY * NC), (row // NC) % NY, row % NC
    yh, z = col // NZ, col % NZ
    tb, half = acts.shape[3], acts.shape[3] // 2

    def at_row(px, py, pc):
        return (px * (NY * NC) + py * NC + pc, col)

    def at_col(ph, pz):
        return (row, ph * NZ + pz)

    xs = [at_row((x + d) % NX, yl, core) for d in range(1, NX)]
    ys = [at_row(x, (yl + d) % NY, core) for d in range(1, NY)]
    sibling = at_row(x, yl, 1 - core)
    ahead, behind = at_col(yh, (z + 1) % NZ), at_col(yh, (z + NZ - 1) % NZ)
    across = at_col(1 - yh, z)

    sent = []

    def push(src, dst, to):
        n = len(sent)
        copy = pltpu.make_async_remote_copy(
            src_ref=src, dst_ref=dst, send_sem=send.at[n], recv_sem=recv.at[n],
            device_id=to, device_id_type=MESH,
        )
        copy.start()
        sent.append(copy)
        return copy

    def landed(copies):
        for copy in copies:
            copy.wait_recv()

    mine = x * NY + yl
    loads = [
        (go_ref, go_all.at[mine, core]), (tok_ref, tok_all.at[mine, core]),
        (gate_ref, acts.at[0, yh, z]), (up_ref, acts.at[1, yh, z]),
        (wd_ref, wd), (wg_ref, wg), (wu_ref, wu),
    ]
    loads = [pltpu.make_async_copy(s, d, here.at[i]) for i, (s, d) in enumerate(loads)]
    for load in loads:
        load.start()

    barrier = pltpu.get_barrier_semaphore()
    partners = xs + ys + [sibling, ahead, behind, across]
    for to in partners:
        pl.semaphore_signal(barrier, inc=1, device_id=to, device_id_type=MESH)
    pl.semaphore_wait(barrier, len(partners))

    def ring_send(block, step, first=None):
        copies = []
        for k in range(2):
            for way, to in ((1, ahead), (-1, behind)):
                at = (z + (NZ - way * (step - 1))) % NZ
                src = block(k, at) if first is None else first[k]
                dst = block(k, at)
                if step == NZ // 2:
                    rows = pl.ds(0 if way == 1 else half, half)
                    src, dst = src.at[rows], dst.at[rows]
                copies.append(push(src, dst, to))
        return copies

    def ring_pass(block, step, before):
        copies = []
        for k in range(2):
            for w, (way, to) in enumerate(((1, ahead), (-1, behind))):
                before[2 * k + w].wait_recv()
                at = (z + (NZ - way * (step - 1))) % NZ
                ref = block(k, at)
                if step == NZ // 2:
                    ref = ref.at[pl.ds(0 if way == 1 else half, half)]
                copies.append(push(ref, ref, to))
        return copies

    def own_act(k, at):
        return acts.at[k, yh, at]

    def other_act(k, at):
        return acts.at[k, 1 - yh, at]

    def grad_block(k, at):
        return grad_h.at[k, at]

    def pair_loop(m, step):
        if m in (0, NZ // 2):
            step(m)
        else:
            pl.loop(0, 2)(lambda i: step(m + (NZ - 2 * m) * i))

    def activate(h, m):
        def step(o):
            at = (z + o) % NZ

            @pl.loop(0, tb // ROWS)
            def _(i):
                rows = pl.ds(pl.multiple_of(i * ROWS, ROWS), ROWS)
                g = acts[0, h, at, rows].astype(F32)
                u = acts[1, h, at, rows].astype(F32)
                s = jax.nn.sigmoid(g)
                gs = g * s
                silu[h, at, rows] = gs
                slope[h, at, rows] = u * s * (1.0 + g * (1.0 - s))
                hidden[h, at, rows] = (gs * u).astype(BF16)

        pair_loop(m, step)

    def share(m):
        def step(o):
            at = (z + o) % NZ
            rows = jnp.concatenate(
                [go_all[h * NZ + at].reshape(tb, -1) for h in range(NH)], axis=0
            )
            sums = dot(rows, wd[...], 1, 1)
            for h in range(NH):
                part[h, at] = sums[h * tb : (h + 1) * tb]

        pair_loop(m, step)

    def reduce_step(step, before):
        copies = []
        for h in range(NH):
            for w, (way, to) in enumerate(((1, ahead), (-1, behind))):
                at = (z + (NZ + way * (NZ // 2 + 1 - step))) % NZ
                out = rs_send.at[h, w, step - 1]
                rows = pl.ds(0 if way == 1 else half, half)
                if step == 1:
                    out[rows] = part[h, at, rows].astype(BF16)
                    copies.append(push(out.at[rows], rs_recv.at[h, w, 0, rows], to))
                    continue
                before[2 * h + w].wait_recv()
                if step == 2:
                    rest = pl.ds(half if way == 1 else 0, half)
                    out[rows] = (part[h, at, rows] + rs_recv[h, w, 0, rows].astype(F32)).astype(BF16)
                    out[rest] = part[h, at, rest].astype(BF16)
                else:
                    out[...] = (part[h, at] + rs_recv[h, w, step - 2].astype(F32)).astype(BF16)
                copies.append(push(out, rs_recv.at[h, w, step - 1], to))
        return copies

    def spread(own, copies_of, source):
        return [push(source, own, to) for to in copies_of]

    act1 = ring_send(own_act, 1, first=(gate_ref, up_ref))
    go_y = spread(go_all.at[mine, core], ys, go_ref)
    tok_y = spread(tok_all.at[mine, core], ys, tok_ref)

    def x_line(ref):
        return ref.at[pl.ds(x * NY, NY), core]

    loads[0].wait()
    landed(go_y)
    go_x = spread(x_line(go_all), xs, x_line(go_all))
    act1 = ring_pass(own_act, 2, act1)
    loads[1].wait()
    landed(tok_y)
    tok_x = spread(x_line(tok_all), xs, x_line(tok_all))
    act_y = [push(ref, acts.at[k, yh, z], across) for k, ref in enumerate((gate_ref, up_ref))]
    act1 = ring_pass(own_act, 3, act1)
    landed(go_x)
    go_c = push(go_all.at[:, core], go_all.at[:, core], sibling)
    act1 = ring_pass(own_act, 4, act1)
    loads[4].wait()
    go_c.wait_recv()

    share(4)
    sums = reduce_step(1, None)
    share(3)
    landed(tok_x)
    tok_c = push(tok_all.at[:, core], tok_all.at[:, core], sibling)
    sums = reduce_step(2, sums)
    share(2)
    loads[2].wait()
    loads[3].wait()
    activate(yh, 0)
    activate(yh, 1)
    sums = reduce_step(3, sums)
    share(1)
    share(0)
    activate(yh, 2)
    sums = reduce_step(4, sums)
    landed(act1)
    landed(act_y)
    act2 = ring_send(other_act, 1)
    activate(yh, 3)
    activate(yh, 4)

    swaps = []
    for h in range(NH):
        landed(sums[2 * h : 2 * h + 2])
        total = part[h, z] + rs_recv[h, 0, 3].astype(F32) + rs_recv[h, 1, 3].astype(F32)
        part[h, z] = total
        swap_send[h] = total.astype(BF16)
        swaps.append(push(swap_send.at[h], swap_recv.at[h], across))
    tok_c.wait_recv()
    tok_t[...] = tok_all[...].reshape(-1, tok_all.shape[3]).T
    act2 = ring_pass(other_act, 2, act2)
    activate(1 - yh, 0)
    for h in range(NH):
        swaps[h].wait_recv()
        grad_h[h, z] = (part[h, z] + swap_recv[h].astype(F32)).astype(BF16)
    grads = ring_send(grad_block, 1)
    act2 = ring_pass(other_act, 3, act2)
    activate(1 - yh, 1)
    loads[5].wait()
    loads[6].wait()

    def gradients(m):
        def step(o):
            at = (z + o) % NZ
            for h in range(NH):

                @pl.loop(0, tb // ROWS)
                def _(i):
                    rows = pl.ds(pl.multiple_of(i * ROWS, ROWS), ROWS)
                    gh = grad_h[h, at, rows].astype(F32)
                    gate_grad[h, at, rows] = (gh * slope[h, at, rows]).astype(BF16)
                    up_grad[h, at, rows] = (gh * silu[h, at, rows]).astype(BF16)

            sums = dot(gate_grad[:, at].reshape(NH * tb, -1), wg[...], 1, 1)
            sums += dot(up_grad[:, at].reshape(NH * tb, -1), wu[...], 1, 1)
            pair_sum[o] = sums.reshape(pair_sum.shape[1:])
            core_send[o] = pair_sum[o, :, 1 - core]
            core_copy(o).start()

        pair_loop(m, step)

    def core_copy(o):
        return pltpu.make_async_remote_copy(
            src_ref=core_send.at[o], dst_ref=core_recv.at[o], send_sem=core_send_sem.at[o],
            recv_sem=core_recv_sem.at[o], device_id=sibling, device_id_type=MESH,
        )

    def x_copy(o, h, to_x, to_y):
        return pltpu.make_async_remote_copy(
            src_ref=x_send.at[o, h], dst_ref=x_recv.at[x, to_y], send_sem=x_send_sem.at[o, h],
            recv_sem=x_recv_sem.at[to_y, x], device_id=at_row(to_x, yl, core), device_id_type=MESH,
        )

    def target(o, h):
        at = h * NZ + (z + o) % NZ
        return at // NY, at % NY

    def outward(m):
        def step(o):
            core_copy(o).wait_recv()
            for h in range(NH):
                to_x, to_y = target(o, h)
                x_send[o, h] = pair_sum[o, h, core] + core_recv[o, h]

                @pl.when(to_x == x)
                def _():
                    x_own[to_y] = x_send[o, h]

                @pl.when(to_x != x)
                def _():
                    x_copy(o, h, to_x, to_y).start()

        pair_loop(m, step)

    grads = ring_pass(grad_block, 2, grads)
    gradients(0)
    act2 = ring_pass(other_act, 4, act2)
    activate(1 - yh, 2)
    gradients(1)
    grads = ring_pass(grad_block, 3, grads)
    activate(1 - yh, 3)
    outward(0)
    outward(1)
    gradients(2)
    landed(act2)
    activate(1 - yh, 4)
    grads = ring_pass(grad_block, 4, grads)
    outward(2)
    gradients(3)
    go_flat = go_all[...].reshape(-1, go_all.shape[3])
    width = 256
    for n in range(hidden.shape[3] // width):
        cols = pl.ds(n * width, width)
        st_gd[cols] = dot(hidden[..., cols].reshape(-1, width), go_flat, 0, 0).astype(BF16)
    stores = [pltpu.make_async_copy(st_gd, out_gd, here.at[7])]
    stores[0].start()
    outward(3)
    landed(grads)
    gradients(4)
    for i, (grad, stage, out) in enumerate(((gate_grad, st_gg, out_gg), (up_grad, st_gu, out_gu))):
        for n in range(grad.shape[3] // width):
            cols = pl.ds(n * width, width)
            if i == 0 and n == 1:
                outward(4)
            stage[:, cols] = dot(tok_t[...], grad[..., cols].reshape(-1, width), 1, 0).astype(BF16)
        stores.append(pltpu.make_async_copy(stage, out, here.at[8 + i]))
        stores[-1].start()

    def line_sum(to_y):
        total = x_own[to_y]
        for d in range(1, NX):
            src = (x + d) % NX
            pltpu.make_async_remote_copy(
                src_ref=x_send.at[0, 0], dst_ref=x_recv.at[src, to_y], send_sem=x_send_sem.at[0, 0],
                recv_sem=x_recv_sem.at[to_y, src], device_id=sibling, device_id_type=MESH,
            ).wait_recv()
            total = total + x_recv[src, to_y]
        return total

    last = []
    for d in range(1, NY):
        y_send[d - 1] = line_sum((yl + d) % NY)
        last.append(push(y_send.at[d - 1], y_recv.at[d - 1], ys[d - 1]))
    total = line_sum(yl)
    for d in range(1, NY):
        last[d - 1].wait_recv()
        total = total + y_recv[d - 1]
    out_gt[...] = total.astype(BF16)

    for copy in sent:
        copy.wait_send()

    @pl.loop(0, NZ)
    def _(o):
        core_copy(o).wait_send()
        for h in range(NH):
            to_x, to_y = target(o, h)

            @pl.when(to_x != x)
            def _():
                x_copy(o, h, to_x, to_y).wait_send()

    for store in stores:
        store.wait()


def on_device(tokens, grad_out, gate_pre, up_pre, w_gate, w_up, w_down):
    th, dd = tokens.shape
    tb, ff = gate_pre.shape
    nrow, ncol = NX * NY, NH * NZ
    anywhere = pl.BlockSpec(memory_space=pl.ANY)
    vmem = pltpu.VMEM
    dma = pltpu.SemaphoreType.DMA
    out = [
        jax.ShapeDtypeStruct(tokens.shape, BF16),
        jax.ShapeDtypeStruct(w_gate.shape, BF16),
        jax.ShapeDtypeStruct(w_up.shape, BF16),
        jax.ShapeDtypeStruct(w_down.shape, BF16),
    ]
    every = (NH, NZ, tb, ff)
    scratch = [
        vmem((nrow, NC, th, dd), BF16),
        vmem((nrow, NC, th, dd), BF16),
        vmem((2,) + every, BF16),
        vmem((dd, ff), BF16),
        vmem((dd, ff), BF16),
        vmem((ff, dd), BF16),
        vmem(every, F32),
        vmem((NH, 2, 4, tb, ff), BF16),
        vmem((NH, 2, 4, tb, ff), BF16),
        vmem((NH, tb, ff), BF16),
        vmem((NH, tb, ff), BF16),
        vmem(every, BF16),
        vmem(every, F32),
        vmem(every, F32),
        vmem(every, BF16),
        vmem(every, BF16),
        vmem(every, BF16),
        vmem((dd, ncol * tb), BF16),
        vmem((NZ, NH, NC, th, dd), F32),
        vmem((NZ, NH, th, dd), F32),
        vmem((NZ, NH, th, dd), F32),
        vmem((NZ, NH, th, dd), F32),
        vmem((NX, NY, th, dd), F32),
        vmem((NY, th, dd), F32),
        vmem((NY - 1, th, dd), F32),
        vmem((NY - 1, th, dd), F32),
        vmem((dd, ff), BF16),
        vmem((dd, ff), BF16),
        vmem((ff, dd), BF16),
        dma((COPIES,)),
        dma((COPIES,)),
        dma((NZ,)),
        dma((NZ,)),
        dma((NZ, NH)),
        dma((NY, NX)),
        dma((10,)),
    ]
    return tuple(
        pl.pallas_call(
            kernel,
            out_shape=out,
            in_specs=[anywhere] * 7,
            out_specs=[pl.BlockSpec(memory_space=vmem)] + [anywhere] * 3,
            scratch_shapes=scratch,
            compiler_params=pltpu.CompilerParams(
                collective_id=0, has_side_effects=True, vmem_limit_bytes=56 * 2**20
            ),
            cost_estimate=pl.CostEstimate(
                flops=12 * nrow * NC * th * dd * ff, bytes_accessed=8 * dd * ff * 2, transcendentals=ncol * tb * ff
            ),
        )(tokens, grad_out, gate_pre, up_pre, w_gate, w_up, w_down)
    )


def solution(mesh):
    return jax.shard_map(
        on_device,
        mesh=mesh,
        in_specs=(
            P("row", "col"),
            P("row", "col"),
            P("col", "row"),
            P("col", "row"),
            P("col", "row"),
            P("col", "row"),
            P("row", "col"),
        ),
        out_specs=(P("row", "col"), P("col", "row"), P("col", "row"), P("row", "col")),
        check_vma=False,
    )
```

time: 732 us -> 101 us (0.14)
  waiting for transfers between devices: 594 us -> 0 us
  blocking collectives: 99.6 us -> 0 us
  Pallas kernels: 0 us -> 93.3 us
  matrix products: 15.6 us -> 0 us
  between operations: 13.8 us -> 0.64 us
    reduce_scatter x2 -> x0, waiting for transfers between devices: 370 us -> none  [the longest x1 224 us: on_device(): lax.psum_scatter(contract(grad_full, w_down, 1, 1), 'col', scatter_dimens...]
    all_gather x3 -> x0, waiting for transfers between devices: 222 us -> none  [the longest x1 94.7 us: on_device(): lax.all_gather(up_share, 'col', axis=0, tiled=True)]
    all_gather x2 -> x0, blocking collectives: 99.6 us -> none  [the longest x1 50.9 us: on_device(): lax.all_gather(tokens, 'row', axis=0, tiled=True)]
    pallas_call x0 -> x1, Pallas kernels: none -> 93.3 us  [on_device(): pl.pallas_call(kernel, out_shape=out, in_specs=[anywhere] * 7, out_specs=...]
    dot_general x6 -> x0, matrix products: 15.6 us -> none  [contract(): lax.dot_general(left_side, right_side, (((left_dim,), (right_dim,)), ((),...]
  transfers between devices with their start and end apart: 5 -> 0, of which waited for: 5 -> 0; matrix products, arithmetic and copies ran while one was open for 2% -> 0% of each run, Pallas kernels for 0% -> 0%
where the time goes in v1:
time: 101 us; the launch traced here: 99.3 us
  Pallas kernels  93.3 us (92%)
  local copies, waits for them, and re-layouts  5.42 us (5%)
    pallas_call x1, Pallas kernels, on_device(): pl.pallas_call(kernel, out_shape=out, in_specs=[anywhere] * 7, out_specs=...  93.3 us
    unnamed x8, local copies, waits for them, and re-layouts  5.42 us

profile of v1, /device:TPU:1, one launch (start us, length us, event | category | flops | bytes accessed | tf_op | source)
XLA Modules:
  0.0 99.3 jit_solution(5445630850252852794)
XLA Ops:
  0.6 93.3 %shard_map.102 = (bf16[32,384]{1,0:T(8,128)(2,1)}, bf16[384,768]{1,0:T(8,128)(2,1)}, bf16[384,768]{1,0:T(8,128)(2,1)}, bf16[768,384]{1,0:T(8,128)(2,1)}) custom-call(bf16[32,384]{1,0:T(8,128)(2,1)} %tok_ref.1, bf16[32,384]{1,0:T(8,128)(2,1)} %go_ref.1, bf16[64,768]{1,0:T(8,128)(2,1)} %gate_ref.1, bf16[64,768]{1,0:T(8,128)(2,1)} %up_ref.1, ...), custom_call_target="tpu_custom_call" | custom-call | flops 3623878656 | bytes 4718592 | tf_op jit(solution)/shard_map/pallas_call | solution.py:417
  93.9 1.3 %copy.15 = bf16[32,384]{1,0:T(8,128)(2,1)} copy(bf16[32,384]{1,0:T(8,128)(2,1)} %get-tuple-element.8) | data formatting | bytes 49152
  95.2 0.0 copy-start.1
  95.2 2.0 %copy.16 = bf16[384,768]{1,0:T(8,128)(2,1)} copy(bf16[384,768]{1,0:T(8,128)(2,1)} %get-tuple-element.9) | data formatting | bytes 1179648
  97.2 0.0 copy-done.1
  97.2 0.0 copy-start
  97.2 0.8 copy.17
  98.0 0.5 copy-done
  98.5 0.8 copy.18
Async XLA Ops:
  95.2 2.0 %copy-start.1 = (bf16[384,768]{1,0:T(8,128)(2,1)S(1)}, bf16[384,768]{1,0:T(8,128)(2,1)}, u32[]{:S(2)}) copy-start(bf16[384,768]{1,0:T(8,128)(2,1)} %get-tuple-element.10) | copy-start | bytes 1769476
  97.2 1.3 %copy-start = (bf16[768,384]{1,0:T(8,128)(2,1)S(1)}, bf16[768,384]{1,0:T(8,128)(2,1)}, u32[]{:S(2)}) copy-start(bf16[768,384]{1,0:T(8,128)(2,1)} %get-tuple-element.11) | copy-start | bytes 1769476

commit v2 on v1

--- a/solution.py
+++ b/solution.py
@@ -12,8 +12,8 @@
 BF16 = jnp.bfloat16
 NX, NY, NC = 4, 4, 2
 NH, NZ = 2, 8
-ROWS = 16
-COPIES = 110
+ROWS = 32
+COPIES = 94
 
 
 def dot(left, right, left_dim, right_dim):
@@ -28,7 +28,7 @@
     tok_all, go_all, acts, wg, wu, wd, part, rs_send, rs_recv, swap_send, swap_recv,
     grad_h, silu, slope, hidden, gate_grad, up_grad, tok_t, pair_sum, core_send, core_recv,
     x_send, x_recv, x_own, y_send, y_recv, st_gg, st_gu, st_gd,
-    send, recv, core_send_sem, core_recv_sem, x_send_sem, x_recv_sem, here,
+    send, recv, core_send_sem, core_recv_sem, x_send_sem, x_recv_sem, y_send_sem, y_recv_sem, here,
 ):
     row, col = lax.axis_index("row"), lax.axis_index("col")
     x, yl, core = row // (NY * NC), (row // NC) % NY, row % NC
@@ -79,30 +79,22 @@
         pl.semaphore_signal(barrier, inc=1, device_id=to, device_id_type=MESH)
     pl.semaphore_wait(barrier, len(partners))
 
-    def ring_send(block, step, first=None):
+    def ring_send(block, k, step, first=None):
         copies = []
-        for k in range(2):
-            for way, to in ((1, ahead), (-1, behind)):
-                at = (z + (NZ - way * (step - 1))) % NZ
-                src = block(k, at) if first is None else first[k]
-                dst = block(k, at)
-                if step == NZ // 2:
-                    rows = pl.ds(0 if way == 1 else half, half)
-                    src, dst = src.at[rows], dst.at[rows]
-                copies.append(push(src, dst, to))
+        for way, to in ((1, ahead), (-1, behind)):
+            at = (z + (NZ - way * (step - 1))) % NZ
+            ref = block(k, at)
+            if step == NZ // 2:
+                ref = ref.at[pl.ds(0 if way == 1 else half, half)]
+            copies.append(push(ref if first is None else first, ref, to))
         return copies
 
-    def ring_pass(block, step, before):
-        copies = []
-        for k in range(2):
-            for w, (way, to) in enumerate(((1, ahead), (-1, behind))):
-                before[2 * k + w].wait_recv()
-                at = (z + (NZ - way * (step - 1))) % NZ
-                ref = block(k, at)
-                if step == NZ // 2:
-                    ref = ref.at[pl.ds(0 if way == 1 else half, half)]
-                copies.append(push(ref, ref, to))
-        return copies
+    def ring_pass(block, k, step, before):
+        landed(before)
+        return ring_send(block, k, step)
+
+    def both_pass(block, step, before):
+        return [ring_pass(block, k, step, before[k]) for k in range(2)]
 
     def own_act(k, at):
         return acts.at[k, yh, at]
@@ -172,49 +164,55 @@
     def spread(own, copies_of, source):
         return [push(source, own, to) for to in copies_of]
 
-    act1 = ring_send(own_act, 1, first=(gate_ref, up_ref))
-    go_y = spread(go_all.at[mine, core], ys, go_ref)
+    def x_line(ref, px):
+        return ref.at[pl.ds(px * NY, NY), core]
+
+    go_own = go_all.at[mine, core]
+    go_y = spread(go_own, ys, go_ref)
+    go_x = [spread(go_own, xs, go_ref)]
+    act1 = [ring_send(own_act, k, 1, first=ref) for k, ref in enumerate((gate_ref, up_ref))]
     tok_y = spread(tok_all.at[mine, core], ys, tok_ref)
-
-    def x_line(ref):
-        return ref.at[pl.ds(x * NY, NY), core]
-
+    for d in range(1, NY):
+        go_y[d - 1].wait_recv()
+        block = go_all.at[x * NY + (yl + NY - d) % NY, core]
+        go_x.append(spread(block, xs, block))
+    act_y = [push(ref, acts.at[k, yh, z], across) for k, ref in enumerate((gate_ref, up_ref))]
     loads[0].wait()
-    landed(go_y)
-    go_x = spread(x_line(go_all), xs, x_line(go_all))
-    act1 = ring_pass(own_act, 2, act1)
+    go_c = [push(x_line(go_all, x), x_line(go_all, x), sibling)]
+    loads[2].wait()
+    loads[3].wait()
+    activate(yh, 0)
+    act1 = both_pass(own_act, 2, act1)
+    activate(yh, 1)
     loads[1].wait()
     landed(tok_y)
-    tok_x = spread(x_line(tok_all), xs, x_line(tok_all))
-    act_y = [push(ref, acts.at[k, yh, z], across) for k, ref in enumerate((gate_ref, up_ref))]
-    act1 = ring_pass(own_act, 3, act1)
-    landed(go_x)
-    go_c = push(go_all.at[:, core], go_all.at[:, core], sibling)
-    act1 = ring_pass(own_act, 4, act1)
+    for d in (1, 3, 2):
+        landed([copies[d - 1] for copies in go_x])
+        line = x_line(go_all, (x + NX - d) % NX)
+        go_c.append(push(line, line, sibling))
+    tok_x = spread(x_line(tok_all, x), xs, x_line(tok_all, x))
+    act1 = both_pass(own_act, 3, act1)
     loads[4].wait()
-    go_c.wait_recv()
+    landed(go_c)
 
     share(4)
     sums = reduce_step(1, None)
     share(3)
+    act1 = both_pass(own_act, 4, act1)
+    sums = reduce_step(2, sums)
+    share(2)
     landed(tok_x)
     tok_c = push(tok_all.at[:, core], tok_all.at[:, core], sibling)
-    sums = reduce_step(2, sums)
-    share(2)
-    loads[2].wait()
-    loads[3].wait()
-    activate(yh, 0)
-    activate(yh, 1)
+    activate(yh, 2)
     sums = reduce_step(3, sums)
     share(1)
     share(0)
-    activate(yh, 2)
     sums = reduce_step(4, sums)
-    landed(act1)
     landed(act_y)
-    act2 = ring_send(other_act, 1)
+    act2 = [ring_send(other_act, k, 1) for k in range(2)]
+    for copies in act1:
+        landed(copies)
     activate(yh, 3)
-    activate(yh, 4)
 
     swaps = []
     for h in range(NH):
@@ -223,22 +221,26 @@
         part[h, z] = total
         swap_send[h] = total.astype(BF16)
         swaps.append(push(swap_send.at[h], swap_recv.at[h], across))
+    activate(yh, 4)
+    activate(1 - yh, 0)
+    act2 = both_pass(other_act, 2, act2)
     tok_c.wait_recv()
     tok_t[...] = tok_all[...].reshape(-1, tok_all.shape[3]).T
-    act2 = ring_pass(other_act, 2, act2)
-    activate(1 - yh, 0)
-    for h in range(NH):
+    activate(1 - yh, 1)
+    act2 = both_pass(other_act, 3, act2)
+    activate(1 - yh, 2)
+    loads[5].wait()
+    loads[6].wait()
+
+    def grad_start(h):
         swaps[h].wait_recv()
         grad_h[h, z] = (part[h, z] + swap_recv[h].astype(F32)).astype(BF16)
-    grads = ring_send(grad_block, 1)
-    act2 = ring_pass(other_act, 3, act2)
-    activate(1 - yh, 1)
-    loads[5].wait()
-    loads[6].wait()
+        return ring_send(grad_block, h, 1)
 
     def gradients(m):
-        def step(o):
-            at = (z + o) % NZ
+        offsets = (m,) if m in (0, NZ // 2) else (m, NZ - m)
+        places = [(z + o) % NZ for o in offsets]
+        for at in places:
             for h in range(NH):
 
                 @pl.loop(0, tb // ROWS)
@@ -248,13 +250,14 @@
                     gate_grad[h, at, rows] = (gh * slope[h, at, rows]).astype(BF16)
                     up_grad[h, at, rows] = (gh * silu[h, at, rows]).astype(BF16)
 
-            sums = dot(gate_grad[:, at].reshape(NH * tb, -1), wg[...], 1, 1)
-            sums += dot(up_grad[:, at].reshape(NH * tb, -1), wu[...], 1, 1)
-            pair_sum[o] = sums.reshape(pair_sum.shape[1:])
+        def tall(ref):
+            return jnp.concatenate([ref[:, at].reshape(NH * tb, -1) for at in places], axis=0)
+
+        sums = dot(tall(gate_grad), wg[...], 1, 1) + dot(tall(up_grad), wu[...], 1, 1)
+        for n, o in enumerate(offsets):
+            pair_sum[o] = sums[n * NH * tb : (n + 1) * NH * tb].reshape(pair_sum.shape[1:])
             core_send[o] = pair_sum[o, :, 1 - core]
             core_copy(o).start()
-
-        pair_loop(m, step)
 
     def core_copy(o):
         return pltpu.make_async_remote_copy(
@@ -288,40 +291,6 @@
                     x_copy(o, h, to_x, to_y).start()
 
         pair_loop(m, step)
-
-    grads = ring_pass(grad_block, 2, grads)
-    gradients(0)
-    act2 = ring_pass(other_act, 4, act2)
-    activate(1 - yh, 2)
-    gradients(1)
-    grads = ring_pass(grad_block, 3, grads)
-    activate(1 - yh, 3)
-    outward(0)
-    outward(1)
-    gradients(2)
-    landed(act2)
-    activate(1 - yh, 4)
-    grads = ring_pass(grad_block, 4, grads)
-    outward(2)
-    gradients(3)
-    go_flat = go_all[...].reshape(-1, go_all.shape[3])
-    width = 256
-    for n in range(hidden.shape[3] // width):
-        cols = pl.ds(n * width, width)
-        st_gd[cols] = dot(hidden[..., cols].reshape(-1, width), go_flat, 0, 0).astype(BF16)
-    stores = [pltpu.make_async_copy(st_gd, out_gd, here.at[7])]
-    stores[0].start()
-    outward(3)
-    landed(grads)
-    gradients(4)
-    for i, (grad, stage, out) in enumerate(((gate_grad, st_gg, out_gg), (up_grad, st_gu, out_gu))):
-        for n in range(grad.shape[3] // width):
-            cols = pl.ds(n * width, width)
-            if i == 0 and n == 1:
-                outward(4)
-            stage[:, cols] = dot(tok_t[...], grad[..., cols].reshape(-1, width), 1, 0).astype(BF16)
-        stores.append(pltpu.make_async_copy(stage, out, here.at[8 + i]))
-        stores[-1].start()
 
     def line_sum(to_y):
         total = x_own[to_y]
@@ -334,14 +303,67 @@
             total = total + x_recv[src, to_y]
         return total
 
-    last = []
+    def y_copy(e, src, to_y):
+        return pltpu.make_async_remote_copy(
+            src_ref=y_send.at[e], dst_ref=y_recv.at[src], send_sem=y_send_sem.at[e],
+            recv_sem=y_recv_sem.at[src], device_id=at_row(x, to_y, core), device_id_type=MESH,
+        )
+
+    late = z % NY
+
+    def y_start(e):
+        to_y = (late + e) % NY
+        y_send[e] = line_sum(to_y)
+
+        @pl.when(to_y != yl)
+        def _():
+            y_copy(e, yl, to_y).start()
+
+    grads = [grad_start(0)]
+    act2 = both_pass(other_act, 4, act2)
+    activate(1 - yh, 3)
+    grads.append(grad_start(1))
+    gradients(0)
+    grads = both_pass(grad_block, 2, grads)
+    for copies in act2:
+        landed(copies)
+    activate(1 - yh, 4)
+    gradients(1)
+    outward(0)
+    grads = both_pass(grad_block, 3, grads)
+    gradients(2)
+    outward(1)
+    grads = both_pass(grad_block, 4, grads)
+    gradients(3)
+    outward(2)
+    go_flat = go_all[...].reshape(-1, go_all.shape[3])
+    width = 256
+    for n in range(hidden.shape[3] // width):
+        cols = pl.ds(n * width, width)
+        st_gd[cols] = dot(hidden[..., cols].reshape(-1, width), go_flat, 0, 0).astype(BF16)
+    stores = [pltpu.make_async_copy(st_gd, out_gd, here.at[7])]
+    stores[0].start()
+    outward(3)
+    for copies in grads:
+        landed(copies)
+    gradients(4)
+    for e in (2, 1, 3):
+        y_start(e)
+    outward(4)
+    for i, (grad, stage, out) in enumerate(((gate_grad, st_gg, out_gg), (up_grad, st_gu, out_gu))):
+        for n in range(grad.shape[3] // width):
+            cols = pl.ds(n * width, width)
+            if i == 1 and n == 0:
+                y_start(0)
+            stage[:, cols] = dot(tok_t[...], grad[..., cols].reshape(-1, width), 1, 0).astype(BF16)
+        stores.append(pltpu.make_async_copy(stage, out, here.at[8 + i]))
+        stores[-1].start()
+
+    total = y_send[(yl + NY - late) % NY]
     for d in range(1, NY):
-        y_send[d - 1] = line_sum((yl + d) % NY)
-        last.append(push(y_send.at[d - 1], y_recv.at[d - 1], ys[d - 1]))
-    total = line_sum(yl)
-    for d in range(1, NY):
-        last[d - 1].wait_recv()
-        total = total + y_recv[d - 1]
+        src = (yl + d) % NY
+        y_copy(0, src, yl).wait_recv()
+        total = total + y_recv[src]
     out_gt[...] = total.astype(BF16)
 
     for copy in sent:
@@ -357,8 +379,24 @@
             def _():
                 x_copy(o, h, to_x, to_y).wait_send()
 
+    for e in range(NY):
+        to_y = (late + e) % NY
+
+        @pl.when(to_y != yl)
+        def _():
+            y_copy(e, yl, to_y).wait_send()
+
     for store in stores:
         store.wait()
+
+
+def copy_kernel(*refs):
+    sources, results, sems = refs[:4], refs[4:8], refs[8]
+    copies = [pltpu.make_async_copy(s, r, sems.at[i]) for i, (s, r) in enumerate(zip(sources, results))]
+    for copy in copies:
+        copy.start()
+    for copy in copies:
+        copy.wait()
 
 
 def on_device(tokens, grad_out, gate_pre, up_pre, w_gate, w_up, w_down):
@@ -400,8 +438,8 @@
         vmem((NZ, NH, th, dd), F32),
         vmem((NX, NY, th, dd), F32),
         vmem((NY, th, dd), F32),
-        vmem((NY - 1, th, dd), F32),
-        vmem((NY - 1, th, dd), F32),
+        vmem((NY, th, dd), F32),
+        vmem((NY, th, dd), F32),
         vmem((dd, ff), BF16),
         vmem((dd, ff), BF16),
         vmem((ff, dd), BF16),
@@ -411,9 +449,11 @@
         dma((NZ,)),
         dma((NZ, NH)),
         dma((NY, NX)),
+        dma((NY,)),
+        dma((NY,)),
         dma((10,)),
     ]
-    return tuple(
+    results = (
         pl.pallas_call(
             kernel,
             out_shape=out,
@@ -427,6 +467,16 @@
                 flops=12 * nrow * NC * th * dd * ff, bytes_accessed=8 * dd * ff * 2, transcendentals=ncol * tb * ff
             ),
         )(tokens, grad_out, gate_pre, up_pre, w_gate, w_up, w_down)
+    )
+    return tuple(
+        pl.pallas_call(
+            copy_kernel,
+            out_shape=out,
+            in_specs=[anywhere] * 4,
+            out_specs=[anywhere] * 4,
+            scratch_shapes=[dma((4,))],
+            compiler_params=pltpu.CompilerParams(vmem_limit_bytes=60 * 2**20),
+        )(*results)
     )
 
 

time: 101 us -> 154 us (1.52)
  Pallas kernels: 93.3 us -> 151 us
  local copies, waits for them, and re-layouts: 5.42 us -> 0 us
    pallas_call x0 -> x1, Pallas kernels: none -> 55.5 us  [on_device(): pl.pallas_call(copy_kernel, out_shape=out, in_specs=[anywhere] * 4, out_s...]
    unnamed x8 -> x0, local copies, waits for them, and re-layouts: 5.42 us -> none
    pallas_call x1, Pallas kernels: 93.3 us -> 95.8 us  [on_device(): pl.pallas_call(kernel, out_shape=out, in_specs=[anywhere] * 7, out_specs=...]
where the time goes in v2:
time: 154 us; the launch traced here: 152 us
  Pallas kernels  151 us (98%)
    pallas_call x1, Pallas kernels, on_device(): pl.pallas_call(kernel, out_shape=out, in_specs=[anywhere] * 7, out_specs=...  95.8 us
    pallas_call x1, Pallas kernels, on_device(): pl.pallas_call(copy_kernel, out_shape=out, in_specs=[anywhere] * 4, out_s...  55.5 us

profile of v2, /device:TPU:1, one launch (start us, length us, event | category | flops | bytes accessed | tf_op | source)
XLA Modules:
  0.0 151.9 jit_solution(13414895936985902747)
XLA Ops:
  0.6 95.8 %shard_map.102 = (bf16[32,384]{1,0:T(8,128)(2,1)}, bf16[384,768]{1,0:T(8,128)(2,1)}, bf16[384,768]{1,0:T(8,128)(2,1)}, bf16[768,384]{1,0:T(8,128)(2,1)}) custom-call(bf16[32,384]{1,0:T(8,128)(2,1)} %tok_ref.1, bf16[32,384]{1,0:T(8,128)(2,1)} %go_ref.1, bf16[64,768]{1,0:T(8,128)(2,1)} %gate_ref.1, bf16[64,768]{1,0:T(8,128)(2,1)} %up_ref.1, ...), custom_call_target="tpu_custom_call" | custom-call | flops 3623878656 | bytes 4718592 | tf_op jit(solution)/shard_map/pallas_call | solution.py:457
  96.5 55.5 %shard_map.103 = (bf16[32,384]{1,0:T(8,128)(2,1)}, bf16[384,768]{1,0:T(8,128)(2,1)}, bf16[384,768]{1,0:T(8,128)(2,1)}, bf16[768,384]{1,0:T(8,128)(2,1)}) custom-call(bf16[32,384]{1,0:T(8,128)(2,1)} %get-tuple-element.8.refs_0_, bf16[384,768]{1,0:T(8,128)(2,1)} %get-tuple-element.9.refs_1_, bf16[384,768]{1,0:T(8,128)(2,1)} %get-tuple-element.10.refs_2_, ...), custom_call_target="tpu_custom_call" | custom-call | tf_op jit(solution)/shard_map/pallas_call | solution.py:472

commit v3 on v2

--- a/solution.py
+++ b/solution.py
@@ -347,13 +347,14 @@
     for copies in grads:
         landed(copies)
     gradients(4)
-    for e in (2, 1, 3):
-        y_start(e)
-    outward(4)
     for i, (grad, stage, out) in enumerate(((gate_grad, st_gg, out_gg), (up_grad, st_gu, out_gu))):
         for n in range(grad.shape[3] // width):
             cols = pl.ds(n * width, width)
-            if i == 1 and n == 0:
+            if i == 0 and n == 1:
+                outward(4)
+                for e in (2, 1, 3):
+                    y_start(e)
+            if i == 1 and n == 1:
                 y_start(0)
             stage[:, cols] = dot(tok_t[...], grad[..., cols].reshape(-1, width), 1, 0).astype(BF16)
         stores.append(pltpu.make_async_copy(stage, out, here.at[8 + i]))
@@ -391,12 +392,16 @@
 
 
 def copy_kernel(*refs):
-    sources, results, sems = refs[:4], refs[4:8], refs[8]
-    copies = [pltpu.make_async_copy(s, r, sems.at[i]) for i, (s, r) in enumerate(zip(sources, results))]
-    for copy in copies:
-        copy.start()
-    for copy in copies:
-        copy.wait()
+    sources, results, held, sems = refs[:4], refs[4:8], refs[8:12], refs[12]
+    reads = [pltpu.make_async_copy(s, h, sems.at[0, i]) for i, (s, h) in enumerate(zip(sources, held))]
+    writes = [pltpu.make_async_copy(h, r, sems.at[1, i]) for i, (h, r) in enumerate(zip(held, results))]
+    for read in reads:
+        read.start()
+    for read, write in zip(reads, writes):
+        read.wait()
+        write.start()
+    for write in writes:
+        write.wait()
 
 
 def on_device(tokens, grad_out, gate_pre, up_pre, w_gate, w_up, w_down):
@@ -474,7 +479,7 @@
             out_shape=out,
             in_specs=[anywhere] * 4,
             out_specs=[anywhere] * 4,
-            scratch_shapes=[dma((4,))],
+            scratch_shapes=[vmem(o.shape, o.dtype) for o in out] + [dma((2, 4))],
             compiler_params=pltpu.CompilerParams(vmem_limit_bytes=60 * 2**20),
         )(*results)
     )

time: 154 us -> 99.3 us (0.64)
  Pallas kernels: 151 us -> 98.1 us
    pallas_call x1, Pallas kernels: 55.5 us -> 2.36 us  [on_device(): pl.pallas_call(copy_kernel, out_shape=out, in_specs=[anywhere] * 4, out_s...]
where the time goes in v3:
time: 99.3 us; the launch traced here: 98.8 us
  Pallas kernels  98.1 us (99%)
    pallas_call x1, Pallas kernels, on_device(): pl.pallas_call(kernel, out_shape=out, in_specs=[anywhere] * 7, out_specs=...  95.8 us
    pallas_call x1, Pallas kernels, on_device(): pl.pallas_call(copy_kernel, out_shape=out, in_specs=[anywhere] * 4, out_s...  2.36 us

profile of v3, /device:TPU:1, one launch (start us, length us, event | category | flops | bytes accessed | tf_op | source)
XLA Modules:
  0.0 98.8 jit_solution(17179336992192618575)
XLA Ops:
  0.6 95.8 %shard_map.102 = (bf16[32,384]{1,0:T(8,128)(2,1)}, bf16[384,768]{1,0:T(8,128)(2,1)}, bf16[384,768]{1,0:T(8,128)(2,1)}, bf16[768,384]{1,0:T(8,128)(2,1)}) custom-call(bf16[32,384]{1,0:T(8,128)(2,1)} %tok_ref.1, bf16[32,384]{1,0:T(8,128)(2,1)} %go_ref.1, bf16[64,768]{1,0:T(8,128)(2,1)} %gate_ref.1, bf16[64,768]{1,0:T(8,128)(2,1)} %up_ref.1, ...), custom_call_target="tpu_custom_call" | custom-call | flops 3623878656 | bytes 4718592 | tf_op jit(solution)/shard_map/pallas_call | solution.py:462
  96.4 2.4 %shard_map.103 = (bf16[32,384]{1,0:T(8,128)(2,1)}, bf16[384,768]{1,0:T(8,128)(2,1)}, bf16[384,768]{1,0:T(8,128)(2,1)}, bf16[768,384]{1,0:T(8,128)(2,1)}) custom-call(bf16[32,384]{1,0:T(8,128)(2,1)} %get-tuple-element.8.refs_0_, bf16[384,768]{1,0:T(8,128)(2,1)} %get-tuple-element.9.refs_1_, bf16[384,768]{1,0:T(8,128)(2,1)} %get-tuple-element.10.refs_2_, ...), custom_call_target="tpu_custom_call" | custom-call | tf_op jit(solution)/shard_map/pallas_call | solution.py:477

commit v4 on v3

--- a/solution.py
+++ b/solution.py
@@ -13,7 +13,7 @@
 NX, NY, NC = 4, 4, 2
 NH, NZ = 2, 8
 ROWS = 32
-COPIES = 94
+COPIES = 100
 
 
 def dot(left, right, left_dim, right_dim):
@@ -25,7 +25,7 @@
 def kernel(
     tok_ref, go_ref, gate_ref, up_ref, wg_ref, wu_ref, wd_ref,
     out_gt, out_gg, out_gu, out_gd,
-    tok_all, go_all, acts, wg, wu, wd, part, rs_send, rs_recv, swap_send, swap_recv,
+    tok_all, go_all, acts, wg, wu, wd, part, rs_send, rs_recv, swap_send, swap_stop, swap_recv,
     grad_h, silu, slope, hidden, gate_grad, up_grad, tok_t, pair_sum, core_send, core_recv,
     x_send, x_recv, x_own, y_send, y_recv, st_gg, st_gu, st_gd,
     send, recv, core_send_sem, core_recv_sem, x_send_sem, x_recv_sem, y_send_sem, y_recv_sem, here,
@@ -46,6 +46,13 @@
     sibling = at_row(x, yl, 1 - core)
     ahead, behind = at_col(yh, (z + 1) % NZ), at_col(yh, (z + NZ - 1) % NZ)
     across = at_col(1 - yh, z)
+
+    def two_along(turn):
+        return (at_row(x, (yl + 2) % NY, core)[0], ((yh + turn) % NH) * NZ + z)
+
+    turn = (yl + 2) // NY
+    two_up, two_down = two_along(turn), two_along(1 - turn)
+    diagonal = two_along(1)
 
     sent = []
 
@@ -74,7 +81,7 @@
         load.start()
 
     barrier = pltpu.get_barrier_semaphore()
-    partners = xs + ys + [sibling, ahead, behind, across]
+    partners = xs + ys + [sibling, ahead, behind, across, diagonal]
     for to in partners:
         pl.semaphore_signal(barrier, inc=1, device_id=to, device_id_type=MESH)
     pl.semaphore_wait(barrier, len(partners))
@@ -186,19 +193,19 @@
     activate(yh, 1)
     loads[1].wait()
     landed(tok_y)
+    act1 = both_pass(own_act, 3, act1)
     for d in (1, 3, 2):
         landed([copies[d - 1] for copies in go_x])
         line = x_line(go_all, (x + NX - d) % NX)
         go_c.append(push(line, line, sibling))
     tok_x = spread(x_line(tok_all, x), xs, x_line(tok_all, x))
-    act1 = both_pass(own_act, 3, act1)
     loads[4].wait()
     landed(go_c)
 
     share(4)
     sums = reduce_step(1, None)
+    act1 = both_pass(own_act, 4, act1)
     share(3)
-    act1 = both_pass(own_act, 4, act1)
     sums = reduce_step(2, sums)
     share(2)
     landed(tok_x)
@@ -214,26 +221,41 @@
         landed(copies)
     activate(yh, 3)
 
+    def swap_send_on(h, src, dst):
+        copies = []
+        for part_at, to in enumerate((two_up, two_down)):
+            rows = pl.ds(part_at * half, half)
+            copies.append(push(src.at[h, rows], dst.at[h, rows], to))
+        return copies
+
+    def swap_pass(h):
+        copies = []
+        for part_at, to in enumerate((two_up, two_down)):
+            swaps[h][part_at].wait_recv()
+            rows = pl.ds(part_at * half, half)
+            copies.append(push(swap_stop.at[h, rows], swap_recv.at[h, rows], to))
+        swaps[h] = copies
+
     swaps = []
     for h in range(NH):
         landed(sums[2 * h : 2 * h + 2])
         total = part[h, z] + rs_recv[h, 0, 3].astype(F32) + rs_recv[h, 1, 3].astype(F32)
         part[h, z] = total
         swap_send[h] = total.astype(BF16)
-        swaps.append(push(swap_send.at[h], swap_recv.at[h], across))
+        swaps.append(swap_send_on(h, swap_send, swap_stop))
     activate(yh, 4)
     activate(1 - yh, 0)
+    swap_pass(0)
     act2 = both_pass(other_act, 2, act2)
+    swap_pass(1)
     tok_c.wait_recv()
     tok_t[...] = tok_all[...].reshape(-1, tok_all.shape[3]).T
     activate(1 - yh, 1)
-    act2 = both_pass(other_act, 3, act2)
-    activate(1 - yh, 2)
     loads[5].wait()
     loads[6].wait()
 
     def grad_start(h):
-        swaps[h].wait_recv()
+        landed(swaps[h])
         grad_h[h, z] = (part[h, z] + swap_recv[h].astype(F32)).astype(BF16)
         return ring_send(grad_block, h, 1)
 
@@ -320,9 +342,11 @@
             y_copy(e, yl, to_y).start()
 
     grads = [grad_start(0)]
+    act2 = both_pass(other_act, 3, act2)
+    grads.append(grad_start(1))
+    activate(1 - yh, 2)
     act2 = both_pass(other_act, 4, act2)
     activate(1 - yh, 3)
-    grads.append(grad_start(1))
     gradients(0)
     grads = both_pass(grad_block, 2, grads)
     for copies in act2:
@@ -428,6 +452,7 @@
         vmem(every, F32),
         vmem((NH, 2, 4, tb, ff), BF16),
         vmem((NH, 2, 4, tb, ff), BF16),
+        vmem((NH, tb, ff), BF16),
         vmem((NH, tb, ff), BF16),
         vmem((NH, tb, ff), BF16),
         vmem(every, BF16),

time: 99.3 us -> 100 us (level)
  no operation moved by 1% of the time
where the time goes in v4:
time: 100 us; the launch traced here: 99.7 us
  Pallas kernels  99 us (99%)
    pallas_call x1, Pallas kernels, on_device(): pl.pallas_call(kernel, out_shape=out, in_specs=[anywhere] * 7, out_specs=...  96.7 us
    pallas_call x1, Pallas kernels, on_device(): pl.pallas_call(copy_kernel, out_shape=out, in_specs=[anywhere] * 4, out_s...  2.36 us

profile of v4, /device:TPU:1, one launch (start us, length us, event | category | flops | bytes accessed | tf_op | source)
XLA Modules:
  0.0 99.7 jit_solution(4288335601507115222)
XLA Ops:
  0.6 96.7 %shard_map.102 = (bf16[32,384]{1,0:T(8,128)(2,1)}, bf16[384,768]{1,0:T(8,128)(2,1)}, bf16[384,768]{1,0:T(8,128)(2,1)}, bf16[768,384]{1,0:T(8,128)(2,1)}) custom-call(bf16[32,384]{1,0:T(8,128)(2,1)} %tok_ref.1, bf16[32,384]{1,0:T(8,128)(2,1)} %go_ref.1, bf16[64,768]{1,0:T(8,128)(2,1)} %gate_ref.1, bf16[64,768]{1,0:T(8,128)(2,1)} %up_ref.1, ...), custom_call_target="tpu_custom_call" | custom-call | flops 3623878656 | bytes 4718592 | tf_op jit(solution)/shard_map/pallas_call | solution.py:487
  97.3 2.4 %shard_map.103 = (bf16[32,384]{1,0:T(8,128)(2,1)}, bf16[384,768]{1,0:T(8,128)(2,1)}, bf16[384,768]{1,0:T(8,128)(2,1)}, bf16[768,384]{1,0:T(8,128)(2,1)}) custom-call(bf16[32,384]{1,0:T(8,128)(2,1)} %get-tuple-element.8.refs_0_, bf16[384,768]{1,0:T(8,128)(2,1)} %get-tuple-element.9.refs_1_, bf16[384,768]{1,0:T(8,128)(2,1)} %get-tuple-element.10.refs_2_, ...), custom_call_target="tpu_custom_call" | custom-call | tf_op jit(solution)/shard_map/pallas_call | solution.py:502

commit v5 on v3

--- a/solution.py
+++ b/solution.py
@@ -13,7 +13,7 @@
 NX, NY, NC = 4, 4, 2
 NH, NZ = 2, 8
 ROWS = 32
-COPIES = 94
+COPIES = 92
 
 
 def dot(left, right, left_dim, right_dim):
@@ -183,22 +183,27 @@
     loads[3].wait()
     activate(yh, 0)
     act1 = both_pass(own_act, 2, act1)
+
+    def across_send(*offsets):
+        refs = [own_act(k, (z + o) % NZ) for k in range(2) for o in offsets]
+        return [push(ref, ref, across) for ref in refs]
+
+    act_near = across_send(1, NZ - 1)
     activate(yh, 1)
     loads[1].wait()
     landed(tok_y)
+    act1 = both_pass(own_act, 3, act1)
     for d in (1, 3, 2):
         landed([copies[d - 1] for copies in go_x])
         line = x_line(go_all, (x + NX - d) % NX)
         go_c.append(push(line, line, sibling))
     tok_x = spread(x_line(tok_all, x), xs, x_line(tok_all, x))
-    act1 = both_pass(own_act, 3, act1)
     loads[4].wait()
     landed(go_c)
 
     share(4)
     sums = reduce_step(1, None)
     share(3)
-    act1 = both_pass(own_act, 4, act1)
     sums = reduce_step(2, sums)
     share(2)
     landed(tok_x)
@@ -208,10 +213,7 @@
     share(1)
     share(0)
     sums = reduce_step(4, sums)
-    landed(act_y)
-    act2 = [ring_send(other_act, k, 1) for k in range(2)]
-    for copies in act1:
-        landed(copies)
+    act1 = both_pass(own_act, 4, act1)
     activate(yh, 3)
 
     swaps = []
@@ -221,14 +223,18 @@
         part[h, z] = total
         swap_send[h] = total.astype(BF16)
         swaps.append(push(swap_send.at[h], swap_recv.at[h], across))
+    landed(act_y)
+    landed(act_near)
+    act2 = [ring_send(other_act, k, 2) for k in range(2)]
+    for copies in act1:
+        landed(copies)
+    act_far = across_send(NZ // 2)
     activate(yh, 4)
     activate(1 - yh, 0)
-    act2 = both_pass(other_act, 2, act2)
     tok_c.wait_recv()
     tok_t[...] = tok_all[...].reshape(-1, tok_all.shape[3]).T
+    act2 = both_pass(other_act, 3, act2)
     activate(1 - yh, 1)
-    act2 = both_pass(other_act, 3, act2)
-    activate(1 - yh, 2)
     loads[5].wait()
     loads[6].wait()
 
@@ -320,17 +326,18 @@
             y_copy(e, yl, to_y).start()
 
     grads = [grad_start(0)]
-    act2 = both_pass(other_act, 4, act2)
+    grads.append(grad_start(1))
+    activate(1 - yh, 2)
+    for copies in act2:
+        landed(copies)
     activate(1 - yh, 3)
-    grads.append(grad_start(1))
     gradients(0)
     grads = both_pass(grad_block, 2, grads)
-    for copies in act2:
-        landed(copies)
-    activate(1 - yh, 4)
     gradients(1)
     outward(0)
     grads = both_pass(grad_block, 3, grads)
+    landed(act_far)
+    activate(1 - yh, 4)
     gradients(2)
     outward(1)
     grads = both_pass(grad_block, 4, grads)

time: 99.3 us -> 105 us (1.057)
  Pallas kernels: 98.1 us -> 104 us
    pallas_call x1, Pallas kernels: 95.8 us -> 101 us  [on_device(): pl.pallas_call(kernel, out_shape=out, in_specs=[anywhere] * 7, out_specs=...]
where the time goes in v5:
time: 105 us; the launch traced here: 104 us
  Pallas kernels  104 us (99%)
    pallas_call x1, Pallas kernels, on_device(): pl.pallas_call(kernel, out_shape=out, in_specs=[anywhere] * 7, out_specs=...  101 us
    pallas_call x1, Pallas kernels, on_device(): pl.pallas_call(copy_kernel, out_shape=out, in_specs=[anywhere] * 4, out_s...  2.36 us

profile of v5, /device:TPU:1, one launch (start us, length us, event | category | flops | bytes accessed | tf_op | source)
XLA Modules:
  0.0 104.2 jit_solution(1959965853782527699)
XLA Ops:
  0.6 101.2 %shard_map.102 = (bf16[32,384]{1,0:T(8,128)(2,1)}, bf16[384,768]{1,0:T(8,128)(2,1)}, bf16[384,768]{1,0:T(8,128)(2,1)}, bf16[768,384]{1,0:T(8,128)(2,1)}) custom-call(bf16[32,384]{1,0:T(8,128)(2,1)} %tok_ref.1, bf16[32,384]{1,0:T(8,128)(2,1)} %go_ref.1, bf16[64,768]{1,0:T(8,128)(2,1)} %gate_ref.1, bf16[64,768]{1,0:T(8,128)(2,1)} %up_ref.1, ...), custom_call_target="tpu_custom_call" | custom-call | flops 3623878656 | bytes 4718592 | tf_op jit(solution)/shard_map/pallas_call | solution.py:469
  101.9 2.4 %shard_map.103 = (bf16[32,384]{1,0:T(8,128)(2,1)}, bf16[384,768]{1,0:T(8,128)(2,1)}, bf16[384,768]{1,0:T(8,128)(2,1)}, bf16[768,384]{1,0:T(8,128)(2,1)}) custom-call(bf16[32,384]{1,0:T(8,128)(2,1)} %get-tuple-element.8.refs_0_, bf16[384,768]{1,0:T(8,128)(2,1)} %get-tuple-element.9.refs_1_, bf16[384,768]{1,0:T(8,128)(2,1)} %get-tuple-element.10.refs_2_, ...), custom_call_target="tpu_custom_call" | custom-call | tf_op jit(solution)/shard_map/pallas_call | solution.py:484

commit v6 on v3

--- a/solution.py
+++ b/solution.py
@@ -13,7 +13,18 @@
 NX, NY, NC = 4, 4, 2
 NH, NZ = 2, 8
 ROWS = 32
-COPIES = 94
+COPIES = 82
+ORDER = (
+    ("a", 1, 0, 1), ("a", 1, 1, 1), ("goy",), ("toky",), ("gox",), ("a", 1, 0, 2), ("a", 1, 1, 2), ("tokx",),
+    ("acty",), ("a", 1, 0, 3), ("a", 1, 1, 3), ("goc",), ("a", 1, 0, 4), ("a", 1, 1, 4), ("S", 4),
+    ("r", 0, 1), ("r", 1, 1), ("S", 3), ("tokc",), ("r", 0, 2), ("r", 1, 2), ("S", 2), ("A", 1, 0),
+    ("A", 1, 1), ("r", 0, 3), ("r", 1, 3), ("S", 1), ("S", 0), ("A", 1, 2), ("r", 0, 4), ("r", 1, 4),
+    ("a", 2, 0, 1), ("a", 2, 1, 1), ("A", 1, 3), ("A", 1, 4), ("w", 0), ("w", 1), ("T",), ("a", 2, 0, 2),
+    ("a", 2, 1, 2), ("A", 2, 0), ("g", 0, 1), ("g", 1, 1), ("a", 2, 0, 3), ("a", 2, 1, 3), ("A", 2, 1),
+    ("g", 0, 2), ("g", 1, 2), ("G", 0), ("a", 2, 0, 4), ("a", 2, 1, 4), ("A", 2, 2), ("G", 1), ("g", 0, 3),
+    ("g", 1, 3), ("A", 2, 3), ("O", 0), ("O", 1), ("G", 2), ("A", 2, 4), ("g", 0, 4), ("g", 1, 4), ("O", 2),
+    ("G", 3), ("D",), ("O", 3), ("G", 4),
+)
 
 
 def dot(left, right, left_dim, right_dim):
@@ -27,7 +38,7 @@
     out_gt, out_gg, out_gu, out_gd,
     tok_all, go_all, acts, wg, wu, wd, part, rs_send, rs_recv, swap_send, swap_recv,
     grad_h, silu, slope, hidden, gate_grad, up_grad, tok_t, pair_sum, core_send, core_recv,
-    x_send, x_recv, x_own, y_send, y_recv, st_gg, st_gu, st_gd,
+    x_send, x_recv, x_late_send, x_late_recv, x_own, y_send, y_recv, y_late_send, y_late_recv, st_gg, st_gu, st_gd,
     send, recv, core_send_sem, core_recv_sem, x_send_sem, x_recv_sem, y_send_sem, y_recv_sem, here,
 ):
     row, col = lax.axis_index("row"), lax.axis_index("col")
@@ -48,6 +59,7 @@
     across = at_col(1 - yh, z)
 
     sent = []
+    coming = {}
 
     def push(src, dst, to):
         n = len(sent)
@@ -59,9 +71,16 @@
         sent.append(copy)
         return copy
 
-    def landed(copies):
-        for copy in copies:
+    def arrive(*key):
+        for copy in coming[key]:
             copy.wait_recv()
+        coming[key] = ()
+
+    def loaded(*which):
+        for i in which:
+            if loads[i] is not None:
+                loads[i].wait()
+                loads[i] = None
 
     mine = x * NY + yl
     loads = [
@@ -89,13 +108,6 @@
             copies.append(push(ref if first is None else first, ref, to))
         return copies
 
-    def ring_pass(block, k, step, before):
-        landed(before)
-        return ring_send(block, k, step)
-
-    def both_pass(block, step, before):
-        return [ring_pass(block, k, step, before[k]) for k in range(2)]
-
     def own_act(k, at):
         return acts.at[k, yh, at]
 
@@ -111,7 +123,16 @@
         else:
             pl.loop(0, 2)(lambda i: step(m + (NZ - 2 * m) * i))
 
-    def activate(h, m):
+    def activate(ring, m):
+        h = yh if ring == 1 else 1 - yh
+        if m == 0 and ring == 1:
+            loaded(2, 3)
+        elif m == 0:
+            arrive("act_y")
+        else:
+            arrive("act", ring, 0, m)
+            arrive("act", ring, 1, m)
+
         def step(o):
             at = (z + o) % NZ
 
@@ -129,6 +150,9 @@
         pair_loop(m, step)
 
     def share(m):
+        arrive("go_core")
+        loaded(4)
+
         def step(o):
             at = (z + o) % NZ
             rows = jnp.concatenate(
@@ -140,106 +164,96 @@
 
         pair_loop(m, step)
 
-    def reduce_step(step, before):
+    def reduce_step(h, step):
         copies = []
-        for h in range(NH):
-            for w, (way, to) in enumerate(((1, ahead), (-1, behind))):
-                at = (z + (NZ + way * (NZ // 2 + 1 - step))) % NZ
-                out = rs_send.at[h, w, step - 1]
-                rows = pl.ds(0 if way == 1 else half, half)
-                if step == 1:
-                    out[rows] = part[h, at, rows].astype(BF16)
-                    copies.append(push(out.at[rows], rs_recv.at[h, w, 0, rows], to))
-                    continue
-                before[2 * h + w].wait_recv()
-                if step == 2:
-                    rest = pl.ds(half if way == 1 else 0, half)
-                    out[rows] = (part[h, at, rows] + rs_recv[h, w, 0, rows].astype(F32)).astype(BF16)
-                    out[rest] = part[h, at, rest].astype(BF16)
-                else:
-                    out[...] = (part[h, at] + rs_recv[h, w, step - 2].astype(F32)).astype(BF16)
-                copies.append(push(out, rs_recv.at[h, w, step - 1], to))
-        return copies
+        for w, (way, to) in enumerate(((1, ahead), (-1, behind))):
+            at = (z + (NZ + way * (NZ // 2 + 1 - step))) % NZ
+            out = rs_send.at[h, w, step - 1]
+            rows = pl.ds(0 if way == 1 else half, half)
+            if step == 1:
+                out[rows] = part[h, at, rows].astype(BF16)
+                copies.append(push(out.at[rows], rs_recv.at[h, w, 0, rows], to))
+                continue
+            coming["sums", h, step - 1][w].wait_recv()
+            if step == 2:
+                rest = pl.ds(half if way == 1 else 0, half)
+                out[rows] = (part[h, at, rows] + rs_recv[h, w, 0, rows].astype(F32)).astype(BF16)
+                out[rest] = part[h, at, rest].astype(BF16)
+            else:
+                out[...] = (part[h, at] + rs_recv[h, w, step - 2].astype(F32)).astype(BF16)
+            copies.append(push(out, rs_recv.at[h, w, step - 1], to))
+        coming["sums", h, step] = copies
 
     def spread(own, copies_of, source):
         return [push(source, own, to) for to in copies_of]
 
-    def x_line(ref, px):
-        return ref.at[pl.ds(px * NY, NY), core]
-
-    go_own = go_all.at[mine, core]
-    go_y = spread(go_own, ys, go_ref)
-    go_x = [spread(go_own, xs, go_ref)]
-    act1 = [ring_send(own_act, k, 1, first=ref) for k, ref in enumerate((gate_ref, up_ref))]
-    tok_y = spread(tok_all.at[mine, core], ys, tok_ref)
-    for d in range(1, NY):
-        go_y[d - 1].wait_recv()
-        block = go_all.at[x * NY + (yl + NY - d) % NY, core]
-        go_x.append(spread(block, xs, block))
-    act_y = [push(ref, acts.at[k, yh, z], across) for k, ref in enumerate((gate_ref, up_ref))]
-    loads[0].wait()
-    go_c = [push(x_line(go_all, x), x_line(go_all, x), sibling)]
-    loads[2].wait()
-    loads[3].wait()
-    activate(yh, 0)
-    act1 = both_pass(own_act, 2, act1)
-    activate(yh, 1)
-    loads[1].wait()
-    landed(tok_y)
-    for d in (1, 3, 2):
-        landed([copies[d - 1] for copies in go_x])
-        line = x_line(go_all, (x + NX - d) % NX)
-        go_c.append(push(line, line, sibling))
-    tok_x = spread(x_line(tok_all, x), xs, x_line(tok_all, x))
-    act1 = both_pass(own_act, 3, act1)
-    loads[4].wait()
-    landed(go_c)
-
-    share(4)
-    sums = reduce_step(1, None)
-    share(3)
-    act1 = both_pass(own_act, 4, act1)
-    sums = reduce_step(2, sums)
-    share(2)
-    landed(tok_x)
-    tok_c = push(tok_all.at[:, core], tok_all.at[:, core], sibling)
-    activate(yh, 2)
-    sums = reduce_step(3, sums)
-    share(1)
-    share(0)
-    sums = reduce_step(4, sums)
-    landed(act_y)
-    act2 = [ring_send(other_act, k, 1) for k in range(2)]
-    for copies in act1:
-        landed(copies)
-    activate(yh, 3)
-
-    swaps = []
-    for h in range(NH):
-        landed(sums[2 * h : 2 * h + 2])
+    def x_line(ref):
+        return ref.at[pl.ds(x * NY, NY), core]
+
+    def go_along_y():
+        coming[("go_y",)] = spread(go_all.at[mine, core], ys, go_ref)
+
+    def go_along_x():
+        loaded(0)
+        arrive("go_y")
+        coming[("go_x",)] = spread(x_line(go_all), xs, x_line(go_all))
+
+    def go_to_core():
+        arrive("go_x")
+        coming[("go_core",)] = [push(go_all.at[:, core], go_all.at[:, core], sibling)]
+
+    def tok_along_y():
+        coming[("tok_y",)] = spread(tok_all.at[mine, core], ys, tok_ref)
+
+    def tok_along_x():
+        loaded(1)
+        arrive("tok_y")
+        coming[("tok_x",)] = spread(x_line(tok_all), xs, x_line(tok_all))
+
+    def tok_to_core():
+        arrive("tok_x")
+        coming[("tok_core",)] = [push(tok_all.at[:, core], tok_all.at[:, core], sibling)]
+
+    def tok_turn():
+        arrive("tok_core")
+        tok_t[...] = tok_all[...].reshape(-1, tok_all.shape[3]).T
+
+    def act_across():
+        refs = enumerate((gate_ref, up_ref))
+        coming[("act_y",)] = [push(ref, acts.at[k, yh, z], across) for k, ref in refs]
+
+    def act_ring(ring, k, step):
+        first = None
+        if step > 1:
+            arrive("act", ring, k, step - 1)
+        elif ring == 1:
+            first = (gate_ref, up_ref)[k]
+        else:
+            arrive("act_y")
+        coming["act", ring, k, step] = ring_send(own_act if ring == 1 else other_act, k, step, first)
+
+    def swap(h):
+        arrive("sums", h, 4)
         total = part[h, z] + rs_recv[h, 0, 3].astype(F32) + rs_recv[h, 1, 3].astype(F32)
         part[h, z] = total
         swap_send[h] = total.astype(BF16)
-        swaps.append(push(swap_send.at[h], swap_recv.at[h], across))
-    activate(yh, 4)
-    activate(1 - yh, 0)
-    act2 = both_pass(other_act, 2, act2)
-    tok_c.wait_recv()
-    tok_t[...] = tok_all[...].reshape(-1, tok_all.shape[3]).T
-    activate(1 - yh, 1)
-    act2 = both_pass(other_act, 3, act2)
-    activate(1 - yh, 2)
-    loads[5].wait()
-    loads[6].wait()
-
-    def grad_start(h):
-        swaps[h].wait_recv()
-        grad_h[h, z] = (part[h, z] + swap_recv[h].astype(F32)).astype(BF16)
-        return ring_send(grad_block, h, 1)
+        coming["swap", h] = [push(swap_send.at[h], swap_recv.at[h], across)]
+
+    def grad_ring(h, step):
+        if step == 1:
+            arrive("swap", h)
+            grad_h[h, z] = (part[h, z] + swap_recv[h].astype(F32)).astype(BF16)
+        else:
+            arrive("grad", h, step - 1)
+        coming["grad", h, step] = ring_send(grad_block, h, step)
 
     def gradients(m):
         offsets = (m,) if m in (0, NZ // 2) else (m, NZ - m)
         places = [(z + o) % NZ for o in offsets]
+        loaded(5, 6)
+        for h in range(NH):
+            if m > 0:
+                arrive("grad", h, m)
         for at in places:
             for h in range(NH):
 
@@ -265,9 +279,18 @@
             recv_sem=core_recv_sem.at[o], device_id=sibling, device_id_type=MESH,
         )
 
+    late = z % NY
+
+    def is_late(o):
+        return o in (0, NZ // 2)
+
     def x_copy(o, h, to_x, to_y):
+        if is_late(o):
+            src, dst = x_late_send.at[o // (NZ // 2), h], x_late_recv.at[x]
+        else:
+            src, dst = x_send.at[o, h], x_recv.at[x, to_y]
         return pltpu.make_async_remote_copy(
-            src_ref=x_send.at[o, h], dst_ref=x_recv.at[x, to_y], send_sem=x_send_sem.at[o, h],
+            src_ref=src, dst_ref=dst, send_sem=x_send_sem.at[o, h],
             recv_sem=x_recv_sem.at[to_y, x], device_id=at_row(to_x, yl, core), device_id_type=MESH,
         )
 
@@ -276,11 +299,14 @@
         return at // NY, at % NY
 
     def outward(m):
-        def step(o):
+        for o in (m,) if is_late(m) else (m, NZ - m):
             core_copy(o).wait_recv()
             for h in range(NH):
                 to_x, to_y = target(o, h)
-                x_send[o, h] = pair_sum[o, h, core] + core_recv[o, h]
+                total = pair_sum[o, h, core] + core_recv[o, h]
+                if is_late(o):
+                    x_late_send[o // (NZ // 2), h] = total.astype(BF16)
+                x_send[o, h] = total
 
                 @pl.when(to_x == x)
                 def _():
@@ -290,63 +316,59 @@
                 def _():
                     x_copy(o, h, to_x, to_y).start()
 
-        pair_loop(m, step)
-
-    def line_sum(to_y):
+    def line_sum(to_y, last):
         total = x_own[to_y]
         for d in range(1, NX):
             src = (x + d) % NX
+            dst = x_late_recv.at[src] if last else x_recv.at[src, to_y]
             pltpu.make_async_remote_copy(
-                src_ref=x_send.at[0, 0], dst_ref=x_recv.at[src, to_y], send_sem=x_send_sem.at[0, 0],
+                src_ref=dst, dst_ref=dst, send_sem=x_send_sem.at[0, 0],
                 recv_sem=x_recv_sem.at[to_y, src], device_id=sibling, device_id_type=MESH,
             ).wait_recv()
-            total = total + x_recv[src, to_y]
+            total = total + dst[...].astype(F32)
         return total
 
     def y_copy(e, src, to_y):
         return pltpu.make_async_remote_copy(
-            src_ref=y_send.at[e], dst_ref=y_recv.at[src], send_sem=y_send_sem.at[e],
+            src_ref=y_late_send if e == 0 else y_send.at[e],
+            dst_ref=y_late_recv.at[src] if e == 0 else y_recv.at[src], send_sem=y_send_sem.at[e],
             recv_sem=y_recv_sem.at[src], device_id=at_row(x, to_y, core), device_id_type=MESH,
         )
 
-    late = z % NY
-
     def y_start(e):
         to_y = (late + e) % NY
-        y_send[e] = line_sum(to_y)
+        total = line_sum(to_y, e == 0)
+        y_send[e] = total
+        if e == 0:
+            y_late_send[...] = total.astype(BF16)
 
         @pl.when(to_y != yl)
         def _():
             y_copy(e, yl, to_y).start()
 
-    grads = [grad_start(0)]
-    act2 = both_pass(other_act, 4, act2)
-    activate(1 - yh, 3)
-    grads.append(grad_start(1))
-    gradients(0)
-    grads = both_pass(grad_block, 2, grads)
-    for copies in act2:
-        landed(copies)
-    activate(1 - yh, 4)
-    gradients(1)
-    outward(0)
-    grads = both_pass(grad_block, 3, grads)
-    gradients(2)
-    outward(1)
-    grads = both_pass(grad_block, 4, grads)
-    gradients(3)
-    outward(2)
-    go_flat = go_all[...].reshape(-1, go_all.shape[3])
     width = 256
-    for n in range(hidden.shape[3] // width):
-        cols = pl.ds(n * width, width)
-        st_gd[cols] = dot(hidden[..., cols].reshape(-1, width), go_flat, 0, 0).astype(BF16)
-    stores = [pltpu.make_async_copy(st_gd, out_gd, here.at[7])]
-    stores[0].start()
-    outward(3)
-    for copies in grads:
-        landed(copies)
-    gradients(4)
+    stores = []
+
+    def keep(stage, out):
+        stores.append(pltpu.make_async_copy(stage, out, here.at[7 + len(stores)]))
+        stores[-1].start()
+
+    def down_grads():
+        go_flat = go_all[...].reshape(-1, go_all.shape[3])
+        for n in range(hidden.shape[3] // width):
+            cols = pl.ds(n * width, width)
+            st_gd[cols] = dot(hidden[..., cols].reshape(-1, width), go_flat, 0, 0).astype(BF16)
+        keep(st_gd, out_gd)
+
+    ops = {
+        "goy": go_along_y, "gox": go_along_x, "goc": go_to_core,
+        "toky": tok_along_y, "tokx": tok_along_x, "tokc": tok_to_core, "T": tok_turn,
+        "acty": act_across, "a": act_ring, "A": activate, "S": share, "r": reduce_step,
+        "w": swap, "g": grad_ring, "G": gradients, "O": outward, "D": down_grads,
+    }
+    for op, *at in ORDER:
+        ops[op](*at)
+
     for i, (grad, stage, out) in enumerate(((gate_grad, st_gg, out_gg), (up_grad, st_gu, out_gu))):
         for n in range(grad.shape[3] // width):
             cols = pl.ds(n * width, width)
@@ -354,24 +376,33 @@
                 outward(4)
                 for e in (2, 1, 3):
                     y_start(e)
-            if i == 1 and n == 1:
+            if i == 1 and n == 0:
                 y_start(0)
             stage[:, cols] = dot(tok_t[...], grad[..., cols].reshape(-1, width), 1, 0).astype(BF16)
-        stores.append(pltpu.make_async_copy(stage, out, here.at[8 + i]))
-        stores[-1].start()
-
-    total = y_send[(yl + NY - late) % NY]
-    for d in range(1, NY):
-        src = (yl + d) % NY
-        y_copy(0, src, yl).wait_recv()
-        total = total + y_recv[src]
-    out_gt[...] = total.astype(BF16)
+        keep(stage, out)
+
+    others = [(yl + d) % NY for d in range(1, NY)]
+
+    @pl.when(yl == late)
+    def _():
+        total = y_send[0]
+        for src in others:
+            y_copy(0, src, yl).wait_recv()
+            total = total + y_late_recv[src].astype(F32)
+        out_gt[...] = total.astype(BF16)
+
+    @pl.when(yl != late)
+    def _():
+        total = y_send[(yl + NY - late) % NY]
+        for src in others:
+            y_copy(1, src, yl).wait_recv()
+            total = total + y_recv[src]
+        out_gt[...] = total.astype(BF16)
 
     for copy in sent:
         copy.wait_send()
 
-    @pl.loop(0, NZ)
-    def _(o):
+    for o in range(NZ):
         core_copy(o).wait_send()
         for h in range(NH):
             to_x, to_y = target(o, h)
@@ -442,9 +473,13 @@
         vmem((NZ, NH, th, dd), F32),
         vmem((NZ, NH, th, dd), F32),
         vmem((NX, NY, th, dd), F32),
+        vmem((2, NH, th, dd), BF16),
+        vmem((NX, th, dd), BF16),
         vmem((NY, th, dd), F32),
         vmem((NY, th, dd), F32),
         vmem((NY, th, dd), F32),
+        vmem((th, dd), BF16),
+        vmem((NY, th, dd), BF16),
         vmem((dd, ff), BF16),
         vmem((dd, ff), BF16),
         vmem((ff, dd), BF16),

time: 99.3 us -> 96 us (0.967)
  Pallas kernels: 98.1 us -> 95.2 us
    pallas_call x1, Pallas kernels: 95.8 us -> 92.9 us  [on_device(): pl.pallas_call(kernel, out_shape=out, in_specs=[anywhere] * 7, out_specs=...]
where the time goes in v6:
time: 96 us; the launch traced here: 95.9 us
  Pallas kernels  95.2 us (99%)
    pallas_call x1, Pallas kernels, on_device(): pl.pallas_call(kernel, out_shape=out, in_specs=[anywhere] * 7, out_specs=...  92.9 us
    pallas_call x1, Pallas kernels, on_device(): pl.pallas_call(copy_kernel, out_shape=out, in_specs=[anywhere] * 4, out_s...  2.36 us

profile of v6, /device:TPU:1, one launch (start us, length us, event | category | flops | bytes accessed | tf_op | source)
XLA Modules:
  0.0 95.9 jit_solution(8100266999994981979)
XLA Ops:
  0.6 92.9 %shard_map.102 = (bf16[32,384]{1,0:T(8,128)(2,1)}, bf16[384,768]{1,0:T(8,128)(2,1)}, bf16[384,768]{1,0:T(8,128)(2,1)}, bf16[768,384]{1,0:T(8,128)(2,1)}) custom-call(bf16[32,384]{1,0:T(8,128)(2,1)} %tok_ref.1, bf16[32,384]{1,0:T(8,128)(2,1)} %go_ref.1, bf16[64,768]{1,0:T(8,128)(2,1)} %gate_ref.1, bf16[64,768]{1,0:T(8,128)(2,1)} %up_ref.1, ...), custom_call_target="tpu_custom_call" | custom-call | flops 3623878656 | bytes 4718592 | tf_op jit(solution)/shard_map/pallas_call | solution.py:497
  93.5 2.4 %shard_map.103 = (bf16[32,384]{1,0:T(8,128)(2,1)}, bf16[384,768]{1,0:T(8,128)(2,1)}, bf16[384,768]{1,0:T(8,128)(2,1)}, bf16[768,384]{1,0:T(8,128)(2,1)}) custom-call(bf16[32,384]{1,0:T(8,128)(2,1)} %get-tuple-element.8.refs_0_, bf16[384,768]{1,0:T(8,128)(2,1)} %get-tuple-element.9.refs_1_, bf16[384,768]{1,0:T(8,128)(2,1)} %get-tuple-element.10.refs_2_, ...), custom_call_target="tpu_custom_call" | custom-call | tf_op jit(solution)/shard_map/pallas_call | solution.py:512

commit v7 on v6

--- a/solution.py
+++ b/solution.py
@@ -15,15 +15,15 @@
 ROWS = 32
 COPIES = 82
 ORDER = (
-    ("a", 1, 0, 1), ("a", 1, 1, 1), ("goy",), ("toky",), ("gox",), ("a", 1, 0, 2), ("a", 1, 1, 2), ("tokx",),
-    ("acty",), ("a", 1, 0, 3), ("a", 1, 1, 3), ("goc",), ("a", 1, 0, 4), ("a", 1, 1, 4), ("S", 4),
-    ("r", 0, 1), ("r", 1, 1), ("S", 3), ("tokc",), ("r", 0, 2), ("r", 1, 2), ("S", 2), ("A", 1, 0),
-    ("A", 1, 1), ("r", 0, 3), ("r", 1, 3), ("S", 1), ("S", 0), ("A", 1, 2), ("r", 0, 4), ("r", 1, 4),
-    ("a", 2, 0, 1), ("a", 2, 1, 1), ("A", 1, 3), ("A", 1, 4), ("w", 0), ("w", 1), ("T",), ("a", 2, 0, 2),
-    ("a", 2, 1, 2), ("A", 2, 0), ("g", 0, 1), ("g", 1, 1), ("a", 2, 0, 3), ("a", 2, 1, 3), ("A", 2, 1),
-    ("g", 0, 2), ("g", 1, 2), ("G", 0), ("a", 2, 0, 4), ("a", 2, 1, 4), ("A", 2, 2), ("G", 1), ("g", 0, 3),
-    ("g", 1, 3), ("A", 2, 3), ("O", 0), ("O", 1), ("G", 2), ("A", 2, 4), ("g", 0, 4), ("g", 1, 4), ("O", 2),
-    ("G", 3), ("D",), ("O", 3), ("G", 4),
+    ("goy",), ("a", 1, 1, 1), ("toky",), ("a", 1, 0, 1), ("gox",), ("a", 1, 1, 2), ("acty",), ("a", 1, 0, 2),
+    ("a", 1, 1, 3), ("goc",), ("a", 1, 0, 3), ("a", 1, 1, 4), ("S", 4), ("r", 1, 1), ("a", 1, 0, 4),
+    ("r", 0, 1), ("tokx",), ("S", 3), ("r", 1, 2), ("r", 0, 2), ("S", 2), ("r", 1, 3), ("S", 1), ("tokc",),
+    ("r", 0, 3), ("r", 1, 4), ("A", 1, 4), ("r", 0, 4), ("S", 0), ("A", 2, 0), ("a", 2, 1, 1), ("w", 1),
+    ("a", 2, 0, 1), ("w", 0), ("A", 1, 2), ("a", 2, 1, 2), ("a", 2, 0, 2), ("g", 1, 1), ("A", 2, 1),
+    ("A", 1, 0), ("a", 2, 1, 3), ("A", 1, 1), ("T",), ("g", 0, 1), ("G", 0), ("g", 1, 2), ("A", 1, 3),
+    ("A", 2, 2), ("g", 0, 2), ("a", 2, 0, 3), ("G", 1), ("g", 1, 3), ("O", 0), ("g", 0, 3), ("G", 2),
+    ("a", 2, 0, 4), ("a", 2, 1, 4), ("O", 1), ("A", 2, 3), ("g", 1, 4), ("O", 2), ("G", 3), ("g", 0, 4),
+    ("A", 2, 4), ("D",), ("O", 3), ("G", 4),
 )
 
 

time: 96 us -> 93.4 us (0.973); the launches traced: 95.9 us -> 92.3 us
  Pallas kernels: 95.2 us -> 91.6 us
    pallas_call x1, Pallas kernels: 92.9 us -> 89.3 us  [on_device(): pl.pallas_call(kernel, out_shape=out, in_specs=[anywhere] * 7, out_specs=...]
where the time goes in v7:
time: 93.4 us; the launch traced here: 92.3 us
  Pallas kernels  91.6 us (98%)
    pallas_call x1, Pallas kernels, on_device(): pl.pallas_call(kernel, out_shape=out, in_specs=[anywhere] * 7, out_specs=...  89.3 us
    pallas_call x1, Pallas kernels, on_device(): pl.pallas_call(copy_kernel, out_shape=out, in_specs=[anywhere] * 4, out_s...  2.36 us

profile of v7, /device:TPU:1, one launch (start us, length us, event | category | flops | bytes accessed | tf_op | source)
XLA Modules:
  0.0 92.3 jit_solution(3799448259931331527)
XLA Ops:
  0.6 89.3 %shard_map.102 = (bf16[32,384]{1,0:T(8,128)(2,1)}, bf16[384,768]{1,0:T(8,128)(2,1)}, bf16[384,768]{1,0:T(8,128)(2,1)}, bf16[768,384]{1,0:T(8,128)(2,1)}) custom-call(bf16[32,384]{1,0:T(8,128)(2,1)} %tok_ref.1, bf16[32,384]{1,0:T(8,128)(2,1)} %go_ref.1, bf16[64,768]{1,0:T(8,128)(2,1)} %gate_ref.1, bf16[64,768]{1,0:T(8,128)(2,1)} %up_ref.1, ...), custom_call_target="tpu_custom_call" | custom-call | flops 3623878656 | bytes 4718592 | tf_op jit(solution)/shard_map/pallas_call | solution.py:497
  89.9 2.4 %shard_map.103 = (bf16[32,384]{1,0:T(8,128)(2,1)}, bf16[384,768]{1,0:T(8,128)(2,1)}, bf16[384,768]{1,0:T(8,128)(2,1)}, bf16[768,384]{1,0:T(8,128)(2,1)}) custom-call(bf16[32,384]{1,0:T(8,128)(2,1)} %get-tuple-element.8.refs_0_, bf16[384,768]{1,0:T(8,128)(2,1)} %get-tuple-element.9.refs_1_, bf16[384,768]{1,0:T(8,128)(2,1)} %get-tuple-element.10.refs_2_, ...), custom_call_target="tpu_custom_call" | custom-call | tf_op jit(solution)/shard_map/pallas_call | solution.py:512

commit v8 on v7

--- a/solution.py
+++ b/solution.py
@@ -12,18 +12,22 @@
 BF16 = jnp.bfloat16
 NX, NY, NC = 4, 4, 2
 NH, NZ = 2, 8
+PIECE = 192
 ROWS = 32
-COPIES = 82
+COPIES = 111
 ORDER = (
-    ("goy",), ("a", 1, 1, 1), ("toky",), ("a", 1, 0, 1), ("gox",), ("a", 1, 1, 2), ("acty",), ("a", 1, 0, 2),
-    ("a", 1, 1, 3), ("goc",), ("a", 1, 0, 3), ("a", 1, 1, 4), ("S", 4), ("r", 1, 1), ("a", 1, 0, 4),
-    ("r", 0, 1), ("tokx",), ("S", 3), ("r", 1, 2), ("r", 0, 2), ("S", 2), ("r", 1, 3), ("S", 1), ("tokc",),
-    ("r", 0, 3), ("r", 1, 4), ("A", 1, 4), ("r", 0, 4), ("S", 0), ("A", 2, 0), ("a", 2, 1, 1), ("w", 1),
-    ("a", 2, 0, 1), ("w", 0), ("A", 1, 2), ("a", 2, 1, 2), ("a", 2, 0, 2), ("g", 1, 1), ("A", 2, 1),
-    ("A", 1, 0), ("a", 2, 1, 3), ("A", 1, 1), ("T",), ("g", 0, 1), ("G", 0), ("g", 1, 2), ("A", 1, 3),
-    ("A", 2, 2), ("g", 0, 2), ("a", 2, 0, 3), ("G", 1), ("g", 1, 3), ("O", 0), ("g", 0, 3), ("G", 2),
-    ("a", 2, 0, 4), ("a", 2, 1, 4), ("O", 1), ("A", 2, 3), ("g", 1, 4), ("O", 2), ("G", 3), ("g", 0, 4),
-    ("A", 2, 4), ("D",), ("O", 3), ("G", 4),
+    ("goy",), ("a", 1, 1, 1), ("acty",), ("a", 1, 0, 1), ("gox",), ("a", 1, 1, 2), ("a", 1, 0, 2), ("goc", 0),
+    ("a", 1, 1, 3), ("a", 1, 0, 3), ("goc", 1), ("a", 1, 1, 4), ("S", 4), ("r", 0, 0, 1), ("r", 0, 1, 1),
+    ("r", 1, 0, 1), ("r", 1, 1, 1), ("S", 0), ("a", 1, 0, 4), ("S", 3), ("r", 0, 0, 2), ("r", 0, 1, 2),
+    ("toky",), ("r", 1, 1, 2), ("S", 2), ("r", 0, 0, 3), ("r", 1, 0, 2), ("S", 1), ("r", 1, 1, 3),
+    ("r", 0, 0, 4), ("tokx",), ("a", 2, 1, 1), ("r", 0, 1, 3), ("r", 1, 1, 4), ("r", 1, 0, 3), ("a", 2, 0, 1),
+    ("w", 0, 0), ("r", 0, 1, 4), ("A", 2, 0), ("w", 1, 1), ("tokc",), ("A", 1, 4), ("g", 0, 0, 1),
+    ("a", 2, 1, 2), ("A", 1, 3), ("r", 1, 0, 4), ("w", 0, 1), ("a", 2, 0, 2), ("A", 1, 1), ("g", 1, 1, 1),
+    ("A", 1, 2), ("A", 1, 0), ("w", 1, 0), ("g", 0, 1, 1), ("a", 2, 1, 3), ("A", 2, 1), ("A", 2, 2),
+    ("g", 0, 1, 2), ("g", 1, 0, 1), ("g", 1, 1, 2), ("G", 0), ("T",), ("g", 0, 0, 2), ("g", 1, 0, 2),
+    ("a", 2, 0, 3), ("G", 1), ("g", 0, 0, 3), ("g", 0, 1, 3), ("g", 1, 1, 3), ("G", 2), ("g", 1, 0, 3),
+    ("A", 2, 3), ("a", 2, 1, 4), ("a", 2, 0, 4), ("O", 1), ("g", 0, 0, 4), ("O", 2), ("g", 1, 1, 4),
+    ("g", 0, 1, 4), ("O", 0), ("g", 1, 0, 4), ("G", 3), ("A", 2, 4), ("D",), ("O", 3), ("G", 4),
 )
 
 
@@ -114,9 +118,6 @@
     def other_act(k, at):
         return acts.at[k, 1 - yh, at]
 
-    def grad_block(k, at):
-        return grad_h.at[k, at]
-
     def pair_loop(m, step):
         if m in (0, NZ // 2):
             step(m)
@@ -150,7 +151,8 @@
         pair_loop(m, step)
 
     def share(m):
-        arrive("go_core")
+        arrive("go_core", 0)
+        arrive("go_core", 1)
         loaded(4)
 
         def step(o):
@@ -164,31 +166,27 @@
 
         pair_loop(m, step)
 
-    def reduce_step(h, step):
-        copies = []
-        for w, (way, to) in enumerate(((1, ahead), (-1, behind))):
+    ways = ((1, ahead), (-1, behind))
+
+    def reduce_step(h, p, step):
+        rows = pl.ds(p * half, half)
+        for w, (way, to) in enumerate(ways):
+            if step == 1 and w != p:
+                continue
             at = (z + (NZ + way * (NZ // 2 + 1 - step))) % NZ
-            out = rs_send.at[h, w, step - 1]
-            rows = pl.ds(0 if way == 1 else half, half)
-            if step == 1:
-                out[rows] = part[h, at, rows].astype(BF16)
-                copies.append(push(out.at[rows], rs_recv.at[h, w, 0, rows], to))
-                continue
-            coming["sums", h, step - 1][w].wait_recv()
-            if step == 2:
-                rest = pl.ds(half if way == 1 else 0, half)
-                out[rows] = (part[h, at, rows] + rs_recv[h, w, 0, rows].astype(F32)).astype(BF16)
-                out[rest] = part[h, at, rest].astype(BF16)
-            else:
-                out[...] = (part[h, at] + rs_recv[h, w, step - 2].astype(F32)).astype(BF16)
-            copies.append(push(out, rs_recv.at[h, w, step - 1], to))
-        coming["sums", h, step] = copies
+            out = rs_send.at[h, w, step - 1, rows]
+            value = part[h, at, rows]
+            if step > 2 or (step == 2 and w == p):
+                arrive("sums", h, p, step - 1, w)
+                value = value + rs_recv[h, w, step - 2, rows].astype(F32)
+            out[...] = value.astype(BF16)
+            coming["sums", h, p, step, w] = [push(out, rs_recv.at[h, w, step - 1, rows], to)]
 
     def spread(own, copies_of, source):
         return [push(source, own, to) for to in copies_of]
 
-    def x_line(ref):
-        return ref.at[pl.ds(x * NY, NY), core]
+    def x_line(ref, away=0):
+        return ref.at[pl.ds((x + away) % NX * NY, NY), core]
 
     def go_along_y():
         coming[("go_y",)] = spread(go_all.at[mine, core], ys, go_ref)
@@ -196,11 +194,13 @@
     def go_along_x():
         loaded(0)
         arrive("go_y")
-        coming[("go_x",)] = spread(x_line(go_all), xs, x_line(go_all))
-
-    def go_to_core():
-        arrive("go_x")
-        coming[("go_core",)] = [push(go_all.at[:, core], go_all.at[:, core], sibling)]
+        copies = spread(x_line(go_all), xs, x_line(go_all))
+        coming["go_x", 0], coming["go_x", 1] = [copies[0], copies[2]], [copies[1]]
+
+    def go_to_core(i):
+        arrive("go_x", i)
+        lines = [x_line(go_all, away) for away in ((0, 1, NX - 1), (NX // 2,))[i]]
+        coming["go_core", i] = [push(line, line, sibling) for line in lines]
 
     def tok_along_y():
         coming[("tok_y",)] = spread(tok_all.at[mine, core], ys, tok_ref)
@@ -232,28 +232,36 @@
             arrive("act_y")
         coming["act", ring, k, step] = ring_send(own_act if ring == 1 else other_act, k, step, first)
 
-    def swap(h):
-        arrive("sums", h, 4)
-        total = part[h, z] + rs_recv[h, 0, 3].astype(F32) + rs_recv[h, 1, 3].astype(F32)
-        part[h, z] = total
-        swap_send[h] = total.astype(BF16)
-        coming["swap", h] = [push(swap_send.at[h], swap_recv.at[h], across)]
-
-    def grad_ring(h, step):
+    def swap(h, p):
+        rows = pl.ds(p * half, half)
+        for w in range(2):
+            arrive("sums", h, p, NZ // 2, w)
+        total = part[h, z, rows] + rs_recv[h, 0, 3, rows].astype(F32) + rs_recv[h, 1, 3, rows].astype(F32)
+        part[h, z, rows] = total
+        swap_send[h, rows] = total.astype(BF16)
+        coming["swap", h, p] = [push(swap_send.at[h, rows], swap_recv.at[h, rows], across)]
+
+    def grad_ring(h, p, step):
+        rows = pl.ds(p * half, half)
         if step == 1:
-            arrive("swap", h)
-            grad_h[h, z] = (part[h, z] + swap_recv[h].astype(F32)).astype(BF16)
-        else:
-            arrive("grad", h, step - 1)
-        coming["grad", h, step] = ring_send(grad_block, h, step)
+            arrive("swap", h, p)
+            grad_h[h, z, rows] = (part[h, z, rows] + swap_recv[h, rows].astype(F32)).astype(BF16)
+        for w, (way, to) in enumerate(ways):
+            if step == NZ // 2 and w != p:
+                continue
+            if step > 1:
+                arrive("grad", h, p, step - 1, w)
+            ref = grad_h.at[h, (z + (NZ - way * (step - 1))) % NZ, rows]
+            coming["grad", h, p, step, w] = [push(ref, ref, to)]
 
     def gradients(m):
         offsets = (m,) if m in (0, NZ // 2) else (m, NZ - m)
         places = [(z + o) % NZ for o in offsets]
         loaded(5, 6)
         for h in range(NH):
-            if m > 0:
-                arrive("grad", h, m)
+            for p, w in ((0, 0), (0, 1), (1, 0), (1, 1)):
+                if m > 0 and not (m == NZ // 2 and w != p):
+                    arrive("grad", h, p, m, w)
         for at in places:
             for h in range(NH):
 
@@ -424,10 +432,14 @@
 
 def copy_kernel(*refs):
     sources, results, held, sems = refs[:4], refs[4:8], refs[8:12], refs[12]
-    reads = [pltpu.make_async_copy(s, h, sems.at[0, i]) for i, (s, h) in enumerate(zip(sources, held))]
-    writes = [pltpu.make_async_copy(h, r, sems.at[1, i]) for i, (h, r) in enumerate(zip(held, results))]
-    for read in reads:
-        read.start()
+    reads, writes = [], []
+    for source, result, hold in zip(sources, results, held):
+        high = min(PIECE, source.shape[0])
+        for at in range(0, source.shape[0], high):
+            rows, n = pl.ds(at, high), len(reads)
+            reads.append(pltpu.make_async_copy(source.at[rows], hold.at[rows], sems.at[0, n]))
+            writes.append(pltpu.make_async_copy(hold.at[rows], result.at[rows], sems.at[1, n]))
+            reads[-1].start()
     for read, write in zip(reads, writes):
         read.wait()
         write.start()
@@ -514,7 +526,7 @@
             out_shape=out,
             in_specs=[anywhere] * 4,
             out_specs=[anywhere] * 4,
-            scratch_shapes=[vmem(o.shape, o.dtype) for o in out] + [dma((2, 4))],
+            scratch_shapes=[vmem(o.shape, o.dtype) for o in out] + [dma((2, 16))],
             compiler_params=pltpu.CompilerParams(vmem_limit_bytes=60 * 2**20),
         )(*results)
     )

time: 93.4 us -> 101 us (1.081)
  Pallas kernels: 91.6 us -> 99.1 us
    pallas_call x1, Pallas kernels: 89.3 us -> 96.6 us  [on_device(): pl.pallas_call(kernel, out_shape=out, in_specs=[anywhere] * 7, out_specs=...]
where the time goes in v8:
time: 101 us; the launch traced here: 99.7 us
  Pallas kernels  99.1 us (98%)
    pallas_call x1, Pallas kernels, on_device(): pl.pallas_call(kernel, out_shape=out, in_specs=[anywhere] * 7, out_specs=...  96.6 us
    pallas_call x1, Pallas kernels, on_device(): pl.pallas_call(copy_kernel, out_shape=out, in_specs=[anywhere] * 4, out_s...  2.46 us

profile of v8, /device:TPU:1, one launch (start us, length us, event | category | flops | bytes accessed | tf_op | source)
XLA Modules:
  0.0 99.7 jit_solution(14546284023171048915)
XLA Ops:
  0.6 96.6 %shard_map.102 = (bf16[32,384]{1,0:T(8,128)(2,1)}, bf16[384,768]{1,0:T(8,128)(2,1)}, bf16[384,768]{1,0:T(8,128)(2,1)}, bf16[768,384]{1,0:T(8,128)(2,1)}) custom-call(bf16[32,384]{1,0:T(8,128)(2,1)} %tok_ref.1, bf16[32,384]{1,0:T(8,128)(2,1)} %go_ref.1, bf16[64,768]{1,0:T(8,128)(2,1)} %gate_ref.1, bf16[64,768]{1,0:T(8,128)(2,1)} %up_ref.1, ...), custom_call_target="tpu_custom_call" | custom-call | flops 3623878656 | bytes 4718592 | tf_op jit(solution)/shard_map/pallas_call | solution.py:509
  97.3 2.5 %shard_map.103 = (bf16[32,384]{1,0:T(8,128)(2,1)}, bf16[384,768]{1,0:T(8,128)(2,1)}, bf16[384,768]{1,0:T(8,128)(2,1)}, bf16[768,384]{1,0:T(8,128)(2,1)}) custom-call(bf16[32,384]{1,0:T(8,128)(2,1)} %get-tuple-element.8.refs_0_, bf16[384,768]{1,0:T(8,128)(2,1)} %get-tuple-element.9.refs_1_, bf16[384,768]{1,0:T(8,128)(2,1)} %get-tuple-element.10.refs_2_, ...), custom_call_target="tpu_custom_call" | custom-call | tf_op jit(solution)/shard_map/pallas_call | solution.py:524

commit v9 on v7

--- a/solution.py
+++ b/solution.py
@@ -13,17 +13,15 @@
 NX, NY, NC = 4, 4, 2
 NH, NZ = 2, 8
 ROWS = 32
-COPIES = 82
+COPIES = 65
 ORDER = (
-    ("goy",), ("a", 1, 1, 1), ("toky",), ("a", 1, 0, 1), ("gox",), ("a", 1, 1, 2), ("acty",), ("a", 1, 0, 2),
-    ("a", 1, 1, 3), ("goc",), ("a", 1, 0, 3), ("a", 1, 1, 4), ("S", 4), ("r", 1, 1), ("a", 1, 0, 4),
-    ("r", 0, 1), ("tokx",), ("S", 3), ("r", 1, 2), ("r", 0, 2), ("S", 2), ("r", 1, 3), ("S", 1), ("tokc",),
-    ("r", 0, 3), ("r", 1, 4), ("A", 1, 4), ("r", 0, 4), ("S", 0), ("A", 2, 0), ("a", 2, 1, 1), ("w", 1),
-    ("a", 2, 0, 1), ("w", 0), ("A", 1, 2), ("a", 2, 1, 2), ("a", 2, 0, 2), ("g", 1, 1), ("A", 2, 1),
-    ("A", 1, 0), ("a", 2, 1, 3), ("A", 1, 1), ("T",), ("g", 0, 1), ("G", 0), ("g", 1, 2), ("A", 1, 3),
-    ("A", 2, 2), ("g", 0, 2), ("a", 2, 0, 3), ("G", 1), ("g", 1, 3), ("O", 0), ("g", 0, 3), ("G", 2),
-    ("a", 2, 0, 4), ("a", 2, 1, 4), ("O", 1), ("A", 2, 3), ("g", 1, 4), ("O", 2), ("G", 3), ("g", 0, 4),
-    ("A", 2, 4), ("D",), ("O", 3), ("G", 4),
+    ("goy",), ("a", 1, 1), ("toky",), ("gox",), ("A", 1, 1), ("tokx",), ("a", 1, 2), ("goc",), ("acty",),
+    ("A", 1, 0), ("S", 4), ("r", 1, 1), ("r", 0, 1), ("S", 3), ("r", 1, 2), ("S", 0), ("r", 0, 2), ("S", 2),
+    ("r", 1, 3), ("r", 0, 3), ("S", 1), ("r", 1, 4), ("r", 0, 4), ("tokc",), ("a", 2, 1), ("w", 1),
+    ("a", 1, 3), ("w", 0), ("T",), ("A", 2, 1), ("g", 1, 1), ("a", 2, 2), ("A", 2, 0), ("A", 1, 2),
+    ("A", 1, 3), ("g", 0, 1), ("G", 0), ("a", 1, 4), ("g", 1, 2), ("A", 2, 2), ("O", 0), ("g", 0, 2),
+    ("G", 1), ("a", 2, 3), ("g", 1, 3), ("A", 1, 4), ("O", 1), ("G", 2), ("g", 0, 3), ("a", 2, 4),
+    ("A", 2, 3), ("O", 2), ("g", 1, 4), ("G", 3), ("g", 0, 4), ("A", 2, 4), ("D",), ("O", 3), ("G", 4),
 )
 
 
@@ -85,7 +83,7 @@
     mine = x * NY + yl
     loads = [
         (go_ref, go_all.at[mine, core]), (tok_ref, tok_all.at[mine, core]),
-        (gate_ref, acts.at[0, yh, z]), (up_ref, acts.at[1, yh, z]),
+        (gate_ref, acts.at[yh, z, 0]), (up_ref, acts.at[yh, z, 1]),
         (wd_ref, wd), (wg_ref, wg), (wu_ref, wu),
     ]
     loads = [pltpu.make_async_copy(s, d, here.at[i]) for i, (s, d) in enumerate(loads)]
@@ -98,24 +96,16 @@
         pl.semaphore_signal(barrier, inc=1, device_id=to, device_id_type=MESH)
     pl.semaphore_wait(barrier, len(partners))
 
-    def ring_send(block, k, step, first=None):
+    def ring_send(block, step):
         copies = []
         for way, to in ((1, ahead), (-1, behind)):
             at = (z + (NZ - way * (step - 1))) % NZ
-            ref = block(k, at)
+            ref = block(at)
             if step == NZ // 2:
-                ref = ref.at[pl.ds(0 if way == 1 else half, half)]
-            copies.append(push(ref if first is None else first, ref, to))
+                rows = pl.ds(0 if way == 1 else half, half)
+                ref = ref.at[:, rows] if len(ref.shape) == 3 else ref.at[rows]
+            copies.append(push(ref, ref, to))
         return copies
-
-    def own_act(k, at):
-        return acts.at[k, yh, at]
-
-    def other_act(k, at):
-        return acts.at[k, 1 - yh, at]
-
-    def grad_block(k, at):
-        return grad_h.at[k, at]
 
     def pair_loop(m, step):
         if m in (0, NZ // 2):
@@ -130,8 +120,7 @@
         elif m == 0:
             arrive("act_y")
         else:
-            arrive("act", ring, 0, m)
-            arrive("act", ring, 1, m)
+            arrive("act", ring, m)
 
         def step(o):
             at = (z + o) % NZ
@@ -139,8 +128,8 @@
             @pl.loop(0, tb // ROWS)
             def _(i):
                 rows = pl.ds(pl.multiple_of(i * ROWS, ROWS), ROWS)
-                g = acts[0, h, at, rows].astype(F32)
-                u = acts[1, h, at, rows].astype(F32)
+                g = acts[h, at, 0, rows].astype(F32)
+                u = acts[h, at, 1, rows].astype(F32)
                 s = jax.nn.sigmoid(g)
                 gs = g * s
                 silu[h, at, rows] = gs
@@ -219,18 +208,19 @@
         tok_t[...] = tok_all[...].reshape(-1, tok_all.shape[3]).T
 
     def act_across():
-        refs = enumerate((gate_ref, up_ref))
-        coming[("act_y",)] = [push(ref, acts.at[k, yh, z], across) for k, ref in refs]
-
-    def act_ring(ring, k, step):
-        first = None
+        loaded(2, 3)
+        ref = acts.at[yh, z]
+        coming[("act_y",)] = [push(ref, ref, across)]
+
+    def act_ring(ring, step):
         if step > 1:
-            arrive("act", ring, k, step - 1)
+            arrive("act", ring, step - 1)
         elif ring == 1:
-            first = (gate_ref, up_ref)[k]
+            loaded(2, 3)
         else:
             arrive("act_y")
-        coming["act", ring, k, step] = ring_send(own_act if ring == 1 else other_act, k, step, first)
+        h = yh if ring == 1 else 1 - yh
+        coming["act", ring, step] = ring_send(lambda at: acts.at[h, at], step)
 
     def swap(h):
         arrive("sums", h, 4)
@@ -245,7 +235,7 @@
             grad_h[h, z] = (part[h, z] + swap_recv[h].astype(F32)).astype(BF16)
         else:
             arrive("grad", h, step - 1)
-        coming["grad", h, step] = ring_send(grad_block, h, step)
+        coming["grad", h, step] = ring_send(lambda at: grad_h.at[h, at], step)
 
     def gradients(m):
         offsets = (m,) if m in (0, NZ // 2) else (m, NZ - m)
@@ -270,13 +260,16 @@
         sums = dot(tall(gate_grad), wg[...], 1, 1) + dot(tall(up_grad), wu[...], 1, 1)
         for n, o in enumerate(offsets):
             pair_sum[o] = sums[n * NH * tb : (n + 1) * NH * tb].reshape(pair_sum.shape[1:])
-            core_send[o] = pair_sum[o, :, 1 - core]
-            core_copy(o).start()
-
-    def core_copy(o):
+            core_send[m, n] = pair_sum[o, :, 1 - core]
+        core_copy(m).start()
+
+    def core_copy(m):
+        src, dst = core_send.at[m], core_recv.at[m]
+        if is_late(m):
+            src, dst = src.at[0], dst.at[0]
         return pltpu.make_async_remote_copy(
-            src_ref=core_send.at[o], dst_ref=core_recv.at[o], send_sem=core_send_sem.at[o],
-            recv_sem=core_recv_sem.at[o], device_id=sibling, device_id_type=MESH,
+            src_ref=src, dst_ref=dst, send_sem=core_send_sem.at[m],
+            recv_sem=core_recv_sem.at[m], device_id=sibling, device_id_type=MESH,
         )
 
     late = z % NY
@@ -299,11 +292,11 @@
         return at // NY, at % NY
 
     def outward(m):
-        for o in (m,) if is_late(m) else (m, NZ - m):
-            core_copy(o).wait_recv()
+        core_copy(m).wait_recv()
+        for n, o in enumerate((m,) if is_late(m) else (m, NZ - m)):
             for h in range(NH):
                 to_x, to_y = target(o, h)
-                total = pair_sum[o, h, core] + core_recv[o, h]
+                total = pair_sum[o, h, core] + core_recv[m, n, h]
                 if is_late(o):
                     x_late_send[o // (NZ // 2), h] = total.astype(BF16)
                 x_send[o, h] = total
@@ -402,8 +395,9 @@
     for copy in sent:
         copy.wait_send()
 
+    for m in range(NZ // 2 + 1):
+        core_copy(m).wait_send()
     for o in range(NZ):
-        core_copy(o).wait_send()
         for h in range(NH):
             to_x, to_y = target(o, h)
 
@@ -452,7 +446,7 @@
     scratch = [
         vmem((nrow, NC, th, dd), BF16),
         vmem((nrow, NC, th, dd), BF16),
-        vmem((2,) + every, BF16),
+        vmem((NH, NZ, 2, tb, ff), BF16),
         vmem((dd, ff), BF16),
         vmem((dd, ff), BF16),
         vmem((ff, dd), BF16),
@@ -469,8 +463,8 @@
         vmem(every, BF16),
         vmem((dd, ncol * tb), BF16),
         vmem((NZ, NH, NC, th, dd), F32),
-        vmem((NZ, NH, th, dd), F32),
-        vmem((NZ, NH, th, dd), F32),
+        vmem((NZ // 2 + 1, 2, NH, th, dd), F32),
+        vmem((NZ // 2 + 1, 2, NH, th, dd), F32),
         vmem((NZ, NH, th, dd), F32),
         vmem((NX, NY, th, dd), F32),
         vmem((2, NH, th, dd), BF16),

time: 93.4 us -> 98 us (1.049)
  Pallas kernels: 91.6 us -> 97.2 us
    pallas_call x1, Pallas kernels: 89.3 us -> 94.8 us  [on_device(): pl.pallas_call(kernel, out_shape=out, in_specs=[anywhere] * 7, out_specs=...]
where the time goes in v9:
time: 98 us; the launch traced here: 97.8 us
  Pallas kernels  97.2 us (99%)
    pallas_call x1, Pallas kernels, on_device(): pl.pallas_call(kernel, out_shape=out, in_specs=[anywhere] * 7, out_specs=...  94.8 us
    pallas_call x1, Pallas kernels, on_device(): pl.pallas_call(copy_kernel, out_shape=out, in_specs=[anywhere] * 4, out_s...  2.36 us

profile of v9, /device:TPU:1, one launch (start us, length us, event | category | flops | bytes accessed | tf_op | source)
XLA Modules:
  0.0 97.8 jit_solution(17205156690162649633)
XLA Ops:
  0.6 94.8 %shard_map.102 = (bf16[32,384]{1,0:T(8,128)(2,1)}, bf16[384,768]{1,0:T(8,128)(2,1)}, bf16[384,768]{1,0:T(8,128)(2,1)}, bf16[768,384]{1,0:T(8,128)(2,1)}) custom-call(bf16[32,384]{1,0:T(8,128)(2,1)} %tok_ref.1, bf16[32,384]{1,0:T(8,128)(2,1)} %go_ref.1, bf16[64,768]{1,0:T(8,128)(2,1)} %gate_ref.1, bf16[64,768]{1,0:T(8,128)(2,1)} %up_ref.1, ...), custom_call_target="tpu_custom_call" | custom-call | flops 3623878656 | bytes 4718592 | tf_op jit(solution)/shard_map/pallas_call | solution.py:491
  95.5 2.4 %shard_map.103 = (bf16[32,384]{1,0:T(8,128)(2,1)}, bf16[384,768]{1,0:T(8,128)(2,1)}, bf16[384,768]{1,0:T(8,128)(2,1)}, bf16[768,384]{1,0:T(8,128)(2,1)}) custom-call(bf16[32,384]{1,0:T(8,128)(2,1)} %get-tuple-element.8.refs_0_, bf16[384,768]{1,0:T(8,128)(2,1)} %get-tuple-element.9.refs_1_, bf16[384,768]{1,0:T(8,128)(2,1)} %get-tuple-element.10.refs_2_, ...), custom_call_target="tpu_custom_call" | custom-call | tf_op jit(solution)/shard_map/pallas_call | solution.py:506

commit v10 on v7

--- a/solution.py
+++ b/solution.py
@@ -15,14 +15,14 @@
 ROWS = 32
 COPIES = 82
 ORDER = (
-    ("goy",), ("a", 1, 1, 1), ("toky",), ("a", 1, 0, 1), ("gox",), ("a", 1, 1, 2), ("acty",), ("a", 1, 0, 2),
-    ("a", 1, 1, 3), ("goc",), ("a", 1, 0, 3), ("a", 1, 1, 4), ("S", 4), ("r", 1, 1), ("a", 1, 0, 4),
-    ("r", 0, 1), ("tokx",), ("S", 3), ("r", 1, 2), ("r", 0, 2), ("S", 2), ("r", 1, 3), ("S", 1), ("tokc",),
-    ("r", 0, 3), ("r", 1, 4), ("A", 1, 4), ("r", 0, 4), ("S", 0), ("A", 2, 0), ("a", 2, 1, 1), ("w", 1),
-    ("a", 2, 0, 1), ("w", 0), ("A", 1, 2), ("a", 2, 1, 2), ("a", 2, 0, 2), ("g", 1, 1), ("A", 2, 1),
-    ("A", 1, 0), ("a", 2, 1, 3), ("A", 1, 1), ("T",), ("g", 0, 1), ("G", 0), ("g", 1, 2), ("A", 1, 3),
-    ("A", 2, 2), ("g", 0, 2), ("a", 2, 0, 3), ("G", 1), ("g", 1, 3), ("O", 0), ("g", 0, 3), ("G", 2),
-    ("a", 2, 0, 4), ("a", 2, 1, 4), ("O", 1), ("A", 2, 3), ("g", 1, 4), ("O", 2), ("G", 3), ("g", 0, 4),
+    ("goy",), ("a", 1, 0, 1), ("A", 1, 0), ("acty",), ("a", 1, 1, 1), ("gox",), ("a", 1, 0, 2),
+    ("a", 1, 1, 2), ("a", 1, 0, 3), ("goc",), ("a", 1, 1, 3), ("A", 1, 1), ("a", 2, 1, 1), ("S", 4),
+    ("r", 1, 1), ("toky",), ("r", 0, 1), ("a", 2, 0, 1), ("S", 2), ("S", 3), ("r", 1, 2), ("tokx",), ("S", 1),
+    ("r", 0, 2), ("r", 1, 3), ("A", 1, 3), ("r", 0, 3), ("r", 1, 4), ("A", 2, 1), ("a", 1, 1, 4), ("r", 0, 4),
+    ("S", 0), ("w", 1), ("a", 2, 1, 2), ("tokc",), ("A", 1, 2), ("a", 1, 0, 4), ("a", 2, 0, 2), ("w", 0),
+    ("a", 2, 1, 3), ("A", 2, 0), ("g", 1, 1), ("T",), ("A", 2, 2), ("g", 0, 1), ("G", 0), ("a", 2, 0, 3),
+    ("A", 1, 4), ("g", 1, 2), ("G", 1), ("g", 0, 2), ("A", 2, 3), ("g", 1, 3), ("O", 0), ("O", 1),
+    ("g", 0, 3), ("G", 2), ("a", 2, 1, 4), ("a", 2, 0, 4), ("g", 1, 4), ("G", 3), ("O", 2), ("g", 0, 4),
     ("A", 2, 4), ("D",), ("O", 3), ("G", 4),
 )
 
@@ -270,13 +270,16 @@
         sums = dot(tall(gate_grad), wg[...], 1, 1) + dot(tall(up_grad), wu[...], 1, 1)
         for n, o in enumerate(offsets):
             pair_sum[o] = sums[n * NH * tb : (n + 1) * NH * tb].reshape(pair_sum.shape[1:])
-            core_send[o] = pair_sum[o, :, 1 - core]
-            core_copy(o).start()
-
-    def core_copy(o):
+            core_send[m, n] = pair_sum[o, :, 1 - core]
+        core_copy(m).start()
+
+    def core_copy(m):
+        src, dst = core_send.at[m], core_recv.at[m]
+        if is_late(m):
+            src, dst = src.at[0], dst.at[0]
         return pltpu.make_async_remote_copy(
-            src_ref=core_send.at[o], dst_ref=core_recv.at[o], send_sem=core_send_sem.at[o],
-            recv_sem=core_recv_sem.at[o], device_id=sibling, device_id_type=MESH,
+            src_ref=src, dst_ref=dst, send_sem=core_send_sem.at[m],
+            recv_sem=core_recv_sem.at[m], device_id=sibling, device_id_type=MESH,
         )
 
     late = z % NY
@@ -299,11 +302,11 @@
         return at // NY, at % NY
 
     def outward(m):
-        for o in (m,) if is_late(m) else (m, NZ - m):
-            core_copy(o).wait_recv()
+        core_copy(m).wait_recv()
+        for n, o in enumerate((m,) if is_late(m) else (m, NZ - m)):
             for h in range(NH):
                 to_x, to_y = target(o, h)
-                total = pair_sum[o, h, core] + core_recv[o, h]
+                total = pair_sum[o, h, core] + core_recv[m, n, h]
                 if is_late(o):
                     x_late_send[o // (NZ // 2), h] = total.astype(BF16)
                 x_send[o, h] = total
@@ -402,8 +405,9 @@
     for copy in sent:
         copy.wait_send()
 
+    for m in range(NZ // 2 + 1):
+        core_copy(m).wait_send()
     for o in range(NZ):
-        core_copy(o).wait_send()
         for h in range(NH):
             to_x, to_y = target(o, h)
 
@@ -469,8 +473,8 @@
         vmem(every, BF16),
         vmem((dd, ncol * tb), BF16),
         vmem((NZ, NH, NC, th, dd), F32),
-        vmem((NZ, NH, th, dd), F32),
-        vmem((NZ, NH, th, dd), F32),
+        vmem((NZ // 2 + 1, 2, NH, th, dd), F32),
+        vmem((NZ // 2 + 1, 2, NH, th, dd), F32),
         vmem((NZ, NH, th, dd), F32),
         vmem((NX, NY, th, dd), F32),
         vmem((2, NH, th, dd), BF16),

time: 93.4 us -> 100 us (1.071)
  Pallas kernels: 91.6 us -> 99 us
    pallas_call x1, Pallas kernels: 89.3 us -> 96.6 us  [on_device(): pl.pallas_call(kernel, out_shape=out, in_specs=[anywhere] * 7, out_specs=...]
where the time goes in v10:
time: 100 us; the launch traced here: 99.6 us
  Pallas kernels  99 us (99%)
    pallas_call x1, Pallas kernels, on_device(): pl.pallas_call(kernel, out_shape=out, in_specs=[anywhere] * 7, out_specs=...  96.6 us
    pallas_call x1, Pallas kernels, on_device(): pl.pallas_call(copy_kernel, out_shape=out, in_specs=[anywhere] * 4, out_s...  2.36 us

profile of v10, /device:TPU:1, one launch (start us, length us, event | category | flops | bytes accessed | tf_op | source)
XLA Modules:
  0.0 99.6 jit_solution(16482949880455974997)
XLA Ops:
  0.6 96.6 %shard_map.102 = (bf16[32,384]{1,0:T(8,128)(2,1)}, bf16[384,768]{1,0:T(8,128)(2,1)}, bf16[384,768]{1,0:T(8,128)(2,1)}, bf16[768,384]{1,0:T(8,128)(2,1)}) custom-call(bf16[32,384]{1,0:T(8,128)(2,1)} %tok_ref.1, bf16[32,384]{1,0:T(8,128)(2,1)} %go_ref.1, bf16[64,768]{1,0:T(8,128)(2,1)} %gate_ref.1, bf16[64,768]{1,0:T(8,128)(2,1)} %up_ref.1, ...), custom_call_target="tpu_custom_call" | custom-call | flops 3623878656 | bytes 4718592 | tf_op jit(solution)/shard_map/pallas_call | solution.py:501
  97.3 2.4 %shard_map.103 = (bf16[32,384]{1,0:T(8,128)(2,1)}, bf16[384,768]{1,0:T(8,128)(2,1)}, bf16[384,768]{1,0:T(8,128)(2,1)}, bf16[768,384]{1,0:T(8,128)(2,1)}) custom-call(bf16[32,384]{1,0:T(8,128)(2,1)} %get-tuple-element.8.refs_0_, bf16[384,768]{1,0:T(8,128)(2,1)} %get-tuple-element.9.refs_1_, bf16[384,768]{1,0:T(8,128)(2,1)} %get-tuple-element.10.refs_2_, ...), custom_call_target="tpu_custom_call" | custom-call | tf_op jit(solution)/shard_map/pallas_call | solution.py:516

commit v11 on v10

--- a/solution.py
+++ b/solution.py
@@ -15,15 +15,15 @@
 ROWS = 32
 COPIES = 82
 ORDER = (
-    ("goy",), ("a", 1, 0, 1), ("A", 1, 0), ("acty",), ("a", 1, 1, 1), ("gox",), ("a", 1, 0, 2),
-    ("a", 1, 1, 2), ("a", 1, 0, 3), ("goc",), ("a", 1, 1, 3), ("A", 1, 1), ("a", 2, 1, 1), ("S", 4),
-    ("r", 1, 1), ("toky",), ("r", 0, 1), ("a", 2, 0, 1), ("S", 2), ("S", 3), ("r", 1, 2), ("tokx",), ("S", 1),
-    ("r", 0, 2), ("r", 1, 3), ("A", 1, 3), ("r", 0, 3), ("r", 1, 4), ("A", 2, 1), ("a", 1, 1, 4), ("r", 0, 4),
-    ("S", 0), ("w", 1), ("a", 2, 1, 2), ("tokc",), ("A", 1, 2), ("a", 1, 0, 4), ("a", 2, 0, 2), ("w", 0),
-    ("a", 2, 1, 3), ("A", 2, 0), ("g", 1, 1), ("T",), ("A", 2, 2), ("g", 0, 1), ("G", 0), ("a", 2, 0, 3),
-    ("A", 1, 4), ("g", 1, 2), ("G", 1), ("g", 0, 2), ("A", 2, 3), ("g", 1, 3), ("O", 0), ("O", 1),
-    ("g", 0, 3), ("G", 2), ("a", 2, 1, 4), ("a", 2, 0, 4), ("g", 1, 4), ("G", 3), ("O", 2), ("g", 0, 4),
-    ("A", 2, 4), ("D",), ("O", 3), ("G", 4),
+    ("goy",), ("a", 1, 1, 1), ("toky",), ("a", 1, 0, 1), ("gox",), ("a", 1, 1, 2), ("a", 1, 0, 2),
+    ("a", 1, 1, 3), ("goc",), ("acty",), ("a", 1, 0, 3), ("a", 1, 1, 4), ("S", 4), ("r", 1, 1),
+    ("a", 1, 0, 4), ("r", 0, 1), ("tokx",), ("S", 3), ("r", 1, 2), ("r", 0, 2), ("S", 2), ("r", 1, 3),
+    ("S", 1), ("tokc",), ("r", 0, 3), ("r", 1, 4), ("A", 1, 4), ("r", 0, 4), ("S", 0), ("A", 2, 0),
+    ("a", 2, 1, 1), ("w", 1), ("a", 2, 0, 1), ("w", 0), ("A", 1, 2), ("a", 2, 1, 2), ("a", 2, 0, 2),
+    ("g", 1, 1), ("A", 2, 1), ("A", 1, 0), ("a", 2, 1, 3), ("A", 1, 1), ("T",), ("g", 0, 1), ("G", 0),
+    ("g", 1, 2), ("A", 1, 3), ("A", 2, 2), ("g", 0, 2), ("a", 2, 0, 3), ("G", 1), ("g", 1, 3), ("O", 0),
+    ("g", 0, 3), ("G", 2), ("a", 2, 0, 4), ("a", 2, 1, 4), ("O", 1), ("A", 2, 3), ("g", 1, 4), ("O", 2),
+    ("G", 3), ("g", 0, 4), ("A", 2, 4), ("D",), ("O", 3), ("G", 4),
 )
 
 

time: 100 us -> 93.3 us (0.933)
  Pallas kernels: 99 us -> 91.6 us
    pallas_call x1, Pallas kernels: 96.6 us -> 89.3 us  [on_device(): pl.pallas_call(kernel, out_shape=out, in_specs=[anywhere] * 7, out_specs=...]
where the time goes in v11:
time: 93.3 us; the launch traced here: 92.3 us
  Pallas kernels  91.6 us (98%)
    pallas_call x1, Pallas kernels, on_device(): pl.pallas_call(kernel, out_shape=out, in_specs=[anywhere] * 7, out_specs=...  89.3 us
    pallas_call x1, Pallas kernels, on_device(): pl.pallas_call(copy_kernel, out_shape=out, in_specs=[anywhere] * 4, out_s...  2.36 us

profile of v11, /device:TPU:1, one launch (start us, length us, event | category | flops | bytes accessed | tf_op | source)
XLA Modules:
  0.0 92.3 jit_solution(6513149530857178334)
XLA Ops:
  0.6 89.3 %shard_map.102 = (bf16[32,384]{1,0:T(8,128)(2,1)}, bf16[384,768]{1,0:T(8,128)(2,1)}, bf16[384,768]{1,0:T(8,128)(2,1)}, bf16[768,384]{1,0:T(8,128)(2,1)}) custom-call(bf16[32,384]{1,0:T(8,128)(2,1)} %tok_ref.1, bf16[32,384]{1,0:T(8,128)(2,1)} %go_ref.1, bf16[64,768]{1,0:T(8,128)(2,1)} %gate_ref.1, bf16[64,768]{1,0:T(8,128)(2,1)} %up_ref.1, ...), custom_call_target="tpu_custom_call" | custom-call | flops 3623878656 | bytes 4718592 | tf_op jit(solution)/shard_map/pallas_call | solution.py:501
  89.9 2.4 %shard_map.103 = (bf16[32,384]{1,0:T(8,128)(2,1)}, bf16[384,768]{1,0:T(8,128)(2,1)}, bf16[384,768]{1,0:T(8,128)(2,1)}, bf16[768,384]{1,0:T(8,128)(2,1)}) custom-call(bf16[32,384]{1,0:T(8,128)(2,1)} %get-tuple-element.8.refs_0_, bf16[384,768]{1,0:T(8,128)(2,1)} %get-tuple-element.9.refs_1_, bf16[384,768]{1,0:T(8,128)(2,1)} %get-tuple-element.10.refs_2_, ...), custom_call_target="tpu_custom_call" | custom-call | tf_op jit(solution)/shard_map/pallas_call | solution.py:516
